TPU v7x, 32 devices: a whole 2x2x4 slice. The times are simulated.
32 devices in a mesh: virt: 8 (over y, x, core), pair: 4 (over z).
Axes of the slice: x: 2, y: 2, z: 4, core: 2. Of those that a mesh axis runs over, the one named last changes fastest.
Arguments:
- amplitudes: float32 [1024, 15360], P('pair', 'virt'), may hold values from -6 to 6
- integrals: float32 [15360, 384], P('virt'), may hold values from -0.125 to 0.125
- tile_mask: int32 [160, 4], P('virt'), may hold values from 0 to 1
- mirror_row: int32 [1024], P('pair'), may hold values from 0 to 255, as said below
Outputs:
- residual: float32 [1024, 384], P('pair', 'virt')
Inputs may be any that keep to these rules, and one draw needn't show every extreme that they name: For the row at local index l on pair index q, mirror_row is the local index of its mirror pair's row on pair index (q + G / 2) mod G, G = 4; the rows of one device map one to one onto the rows of that device, and the mirror of the mirror is the row itself.
All inputs are finite; a program needn't handle non-finite values.
Results may differ from a plain program's by a relative error of at most 0.000092.
Values sent between devices are 32-bit elements; how exact they have to be, the bound alone decides.
No kernel may reach another device: no remote copies, remote signals or barrier semaphores. Data moves between devices by JAX's collectives and lax.ppermute only.
A program may use at most 64 MiB of HBM per device.

v0:
```python
import jax
import jax.numpy as jnp
from jax import lax
from jax.sharding import PartitionSpec as P

TILE = 96


def shifted(block, axis, distance):
    devices = range(lax.axis_size(axis))
    route = [((i - distance) % len(devices), i) for i in devices]
    return lax.ppermute(block, axis, route)


def product(left_side, right_side):
    return jnp.dot(
        left_side, right_side, precision=lax.Precision.HIGHEST, preferred_element_type=jnp.float32
    )


def shards(amplitudes, integrals, tile_mask, mirror_row):
    tile_rows = integrals.shape[0] // TILE
    col_tiles = integrals.shape[1] // TILE
    grown_view = (
        integrals.reshape(tile_rows, TILE, col_tiles, TILE)
        * tile_mask.astype(jnp.float32)[:, None, :, None]
    )
    masked = grown_view.reshape(integrals.shape)
    pair_size = lax.axis_size("pair")
    virt_size = lax.axis_size("virt")
    partial_value = product(amplitudes, masked)
    reduced = lax.psum_scatter(partial_value, "virt", scatter_dimension=1, tiled=True)
    turned = shifted(reduced, "virt", virt_size // 2)
    turned = shifted(turned, "pair", pair_size // 2)
    return reduced + jnp.take(turned, mirror_row, axis=0)


def solution(mesh):
    in_specs = (P("pair", "virt"), P("virt", None), P("virt", None), P("pair"))
    out_specs = P("pair", "virt")
    return jax.shard_map(shards, mesh=mesh, in_specs=in_specs, out_specs=out_specs, check_vma=False)
```

profile of v0, /device:TPU:0, one launch (start us, length us, event | category | flops | bytes accessed | tf_op | source)
XLA Modules:
  0.0 78.7 jit_solution(10240521858129516677)
XLA Ops:
  6.5 0.0 copy-start
  6.5 0.0 reduce-scatter.2.cloned.1.call-start
  6.5 0.8 %convert_element_type.3 = f32[20,4]{0,1:T(4,128)S(1)} convert(s32[20,4]{0,1:T(4,128)} %param.6) | non-fusion elementwise | flops 80 | bytes 640 | tf_op jit(solution)/shard_map/convert_element_type | solution.py:26
  7.4 0.1 copy.5
  7.5 2.4 %mul.11 = f32[20,96,4,96]{3,2,1,0:T(4,128)} broadcast(f32[20,4]{1,0:T(8,128)S(1)} %copy.5), dimensions={0,2} | broadcast | bytes 2949440 | tf_op jit(solution)/shard_map/mul | solution.py:25
  9.9 5.3 %mul.12 = f32[1920,384]{1,0:T(8,128)} reshape(f32[20,96,4,96]{3,2,1,0:T(4,128)} %mul.11) | data formatting | bytes 5898240 | tf_op jit(solution)/shard_map/mul | solution.py:25
  15.2 0.0 copy-done
  15.2 0.0 copy-start.1
  15.2 8.3 %fusion.2 = f32[256,384]{0,1:T(8,128)} fusion(f32[256,1920]{1,0:T(8,128)S(1)} %copy-done, f32[1920,384]{1,0:T(8,128)} %param.5, f32[1920,384]{1,0:T(8,128)} %mul.12), kind=kOutput, calls=%fused_computation.3 | convolution fusion | flops 2265661440 | bytes 8257536 | tf_op jit(solution)/shard_map/dot_general | solution.py:16
  23.5 0.0 reduce-scatter.2.cloned.1.call-update
  23.5 0.0 copy-done.1
  23.5 36.7 %reduce-scatter.2.cloned.1.call-done = f32[256,48]{0,1:T(8,128)} async-done(((f32[256,384]{0,1:T(8,128)}), f32[256,48]{0,1:T(8,128)}) %reduce-scatter.2.cloned.1.call-update) | async-done | bytes 49168 | tf_op jit(solution)/shard_map/reduce_scatter | solution.py:32
  60.2 1.5 %collective-permute-start = (f32[256,48]{0,1:T(8,128)}, f32[256,48]{0,1:T(8,128)S(1)}, u32[]{:S(2)}, u32[]{:S(2)}) collective-permute-start(f32[256,48]{0,1:T(8,128)} %reduce-scatter.2.cloned.1.call-done), channel_id=1, source_target_pairs={{16,0},{20,4},{24,8},{28,12},{0,16},{4,20},{8,24},{12,28},{17,1},{... | collective-permute-start | bytes 147464 | tf_op jit(solution)/shard_map/ppermute | solution.py:12
  61.6 2.8 %collective-permute-done = f32[256,48]{0,1:T(8,128)S(1)} collective-permute-done((f32[256,48]{0,1:T(8,128)}, f32[256,48]{0,1:T(8,128)S(1)}, u32[]{:S(2)}, u32[]{:S(2)}) %collective-permute-start) | collective-permute-done | bytes 49184 | tf_op jit(solution)/shard_map/ppermute | solution.py:12
  64.5 2.4 %collective-permute-start.1 = (f32[256,48]{0,1:T(8,128)S(1)}, f32[256,48]{0,1:T(8,128)S(1)}, u32[]{:S(2)}, u32[]{:S(2)}) collective-permute-start(f32[256,48]{0,1:T(8,128)S(1)} %collective-permute-done), channel_id=1, source_target_pairs={{2,0},{3,1},{0,2},{1,3},{6,4},{7,5},{4,6},{5,7},{10,8},{11,9},{8,1... | collective-permute-start | bytes 147464 | tf_op jit(solution)/shard_map/ppermute | solution.py:12
  66.9 2.6 %collective-permute-done.1 = f32[256,48]{0,1:T(8,128)S(1)} collective-permute-done((f32[256,48]{0,1:T(8,128)S(1)}, f32[256,48]{0,1:T(8,128)S(1)}, u32[]{:S(2)}, u32[]{:S(2)}) %collective-permute-start.1) | collective-permute-done | bytes 49184 | tf_op jit(solution)/shard_map/ppermute | solution.py:12
  69.5 0.1 copy.6
  69.6 0.7 gather_fusion
  70.3 0.1 copy.7
  70.4 1.4 %select_add_fusion = f32[256,48]{0,1:T(8,128)} fusion(f32[256,48]{0,1:T(8,128)} %reduce-scatter.2.cloned.1.call-done, f32[256,48]{0,1:T(8,128)S(1)} %copy.7, pred[256]{0:T(512)(128)(4,1)S(1)} %compare_and_fusion), kind=kLoop, calls=%fused_computation.4 | loop fusion | flops 24576 | bytes 147712 | tf_op jit(solution)/shard_map/add | solution.py:35
  (3 shorter events, 0.0 us)
Async XLA Ops:
  6.5 8.7 %copy-start = (f32[256,1920]{1,0:T(8,128)S(1)}, f32[256,1920]{1,0:T(8,128)}, u32[]{:S(2)}) copy-start(f32[256,1920]{1,0:T(8,128)} %param.4) | copy-start | bytes 5898244
  6.5 53.6 %reduce-scatter.2.cloned.1.call-start = ((), (), s32[]{:S(2)}) async-start(), calls=%async_computation.1 | async-start | bytes 442368 | tf_op jit(solution)/shard_map/reduce_scatter | solution.py:32
  15.2 8.3 %copy-start.1 = (s32[256]{0:T(256)S(1)}, s32[256]{0:T(256)}, u32[]{:S(2)}) copy-start(s32[256]{0:T(256)} %param.7) | copy-start | bytes 3076
  60.2 4.3 %collective-permute-start = (f32[256,48]{0,1:T(8,128)}, f32[256,48]{0,1:T(8,128)S(1)}, u32[]{:S(2)}, u32[]{:S(2)}) collective-permute-start(f32[256,48]{0,1:T(8,128)} %reduce-scatter.2.cloned.1.call-done), channel_id=1, source_target_pairs={{16,0},{20,4},{24,8},{28,12},{0,16},{4,20},{8,24},{12,28},{17,1},{... | collective-permute-start | bytes 147464 | tf_op jit(solution)/shard_map/ppermute | solution.py:12
  64.5 5.0 %collective-permute-start.1 = (f32[256,48]{0,1:T(8,128)S(1)}, f32[256,48]{0,1:T(8,128)S(1)}, u32[]{:S(2)}, u32[]{:S(2)}) collective-permute-start(f32[256,48]{0,1:T(8,128)S(1)} %collective-permute-done), channel_id=1, source_target_pairs={{2,0},{3,1},{0,2},{1,3},{6,4},{7,5},{4,6},{5,7},{10,8},{11,9},{8,1... | collective-permute-start | bytes 147464 | tf_op jit(solution)/shard_map/ppermute | solution.py:12
Sparse Core Ops, SparseCore 0:
  23.6 36.5 reduce-scatter.1
where the time goes:
time: 78.9 us; the launch traced here: 78.7 us
  waiting for transfers between devices  42.1 us (53%)
  between operations  13.4 us (17%)
  local copies, waits for them, and re-layouts  8.72 us (11%)
  matrix products  8.29 us (11%)
  starting transfers between devices  3.87 us (5%)
  other arithmetic  2.27 us (3%)
    reduce_scatter x1, waiting for transfers between devices, shards(): lax.psum_scatter(partial_value, 'virt', scatter_dimension=1, tiled=True)  36.7 us
    dot_general x1, matrix products, product(): jnp.dot(left_side, right_side, precision=lax.Precision.HIGHEST, preferred...  8.29 us
    mul x2, local copies, waits for them, and re-layouts, shards(): integrals.reshape(tile_rows, TILE, col_tiles, TILE)  7.72 us
    ppermute x2, waiting for transfers between devices, shifted(): return lax.ppermute(block, axis, route)  5.41 us
    ppermute x2, starting transfers between devices, shifted(): return lax.ppermute(block, axis, route)  3.87 us
  transfers between devices with their start and end apart: 3, of which 3 were waited for; matrix products, arithmetic and copies ran while one was open for 0% of the time, Pallas kernels for 0%

commit v1 on v0

v1 whole, which is shorter than its diff:
```python
import functools

import jax
import jax.numpy as jnp
from jax import lax
from jax.experimental import pallas as pl
from jax.experimental.pallas import tpu as pltpu
from jax.sharding import PartitionSpec as P

CHUNK = 512
MIB = 1 << 20


def split(x):
    high = x.astype(jnp.bfloat16)
    low = (x - high.astype(jnp.float32)).astype(jnp.bfloat16)
    return high, low


def chunks_of(extent):
    return [(start, min(CHUNK, extent - start)) for start in range(0, extent, CHUNK)]


def ladder_kernel(parts, mask_ref, side_ref, amp_ref, int_ref, out_ref, amp, ints, sems):
    depth, cols = int_ref.shape
    rows = amp_ref.shape[0]
    spans = chunks_of(depth)
    copies = []
    for i, (start, size) in enumerate(spans):
        span = pl.ds(start, size)
        one = pltpu.make_async_copy(amp_ref.at[:, span], amp.at[:, span], sems.at[0, i])
        two = pltpu.make_async_copy(int_ref.at[span, :], ints.at[span, :], sems.at[1, i])
        one.start()
        two.start()
        copies.append((one, two))

    col_tiles, tile_rows = mask_ref.shape
    tile_r, tile_c = depth // tile_rows, cols // col_tiles
    lane = lax.broadcasted_iota(jnp.int32, (1, cols), 1)
    total = jnp.zeros((rows, cols), jnp.float32)
    for (start, size), (one, two) in zip(spans, copies):
        one.wait()
        two.wait()
        pieces = []
        at = start
        while at < start + size:
            t = at // tile_r
            end = min((t + 1) * tile_r, start + size)
            factor = jnp.full((1, cols), mask_ref[0, t].astype(jnp.float32))
            for u in range(1, col_tiles):
                factor = jnp.where(lane >= u * tile_c, mask_ref[u, t].astype(jnp.float32), factor)
            pieces.append(ints[at:end, :] * factor)
            at = end
        masked = jnp.concatenate(pieces, axis=0)
        b_high, b_low = split(masked)
        a_high, a_low = split(amp[:, start:start + size])
        dot = functools.partial(jnp.dot, preferred_element_type=jnp.float32)
        total += dot(a_high, b_high) + dot(a_high, b_low) + dot(a_low, b_high)
    turned = total.T
    block = cols // parts
    for b in range(parts):
        out_ref[(b % 2) ^ side_ref[0], b // 2] = turned[b * block:(b + 1) * block, :]


def ladder(parts, mask, side, amplitudes, integrals):
    rows, depth = amplitudes.shape
    cols = integrals.shape[1]
    count = len(chunks_of(depth))
    return pl.pallas_call(
        functools.partial(ladder_kernel, parts),
        out_shape=jax.ShapeDtypeStruct((2, parts // 2, cols // parts, rows), jnp.float32),
        in_specs=[pl.BlockSpec(memory_space=pltpu.SMEM)] * 2 + [pl.BlockSpec(memory_space=pl.ANY)] * 2,
        out_specs=pl.BlockSpec(memory_space=pltpu.VMEM),
        scratch_shapes=[
            pltpu.VMEM((rows, depth), jnp.float32),
            pltpu.VMEM((depth, cols), jnp.float32),
            pltpu.SemaphoreType.DMA((2, count)),
        ],
        compiler_params=pltpu.CompilerParams(vmem_limit_bytes=40 * MIB),
        name="ladder",
    )(mask, side, amplitudes, integrals)


def finish_kernel(mirror_ref, own_ref, other_ref, out_ref):
    rows = own_ref.shape[1]
    lanes = 128
    for j in range(0, rows, lanes):
        index = jnp.broadcast_to(mirror_ref[:, j:j + lanes], (own_ref.shape[0], lanes))
        local = index % lanes
        picked = jnp.zeros(index.shape, jnp.float32)
        for k in range(0, rows, lanes):
            found = jnp.take_along_axis(other_ref[:, k:k + lanes], local, axis=1)
            picked = jnp.where(index // lanes == k // lanes, found, picked)
        out_ref[:, j:j + lanes] = own_ref[:, j:j + lanes] + picked


def finish(mirror, own, other):
    return pl.pallas_call(
        finish_kernel,
        out_shape=jax.ShapeDtypeStruct(own.shape, own.dtype),
        in_specs=[pl.BlockSpec(memory_space=pltpu.VMEM)] * 3,
        out_specs=pl.BlockSpec(memory_space=pltpu.VMEM),
        name="finish",
    )(mirror, own, other)


def shards(amplitudes, integrals, tile_mask, mirror_row):
    n, g = lax.axis_size("virt"), lax.axis_size("pair")
    v = lax.axis_index("virt")
    side, chip = v % 2, v // 2
    half = n // 2
    both = ladder(n, tile_mask.T, side.reshape(1), amplitudes, integrals)
    arrived = lax.ppermute(both[1], "virt", [(i, i ^ 1) for i in range(n)])
    mine = both[0] + arrived
    reduced = lax.dynamic_index_in_dim(mine, chip, 0, keepdims=False)
    came = []
    for s in range(1, half):
        block = lax.dynamic_index_in_dim(mine, (chip + s) % half, 0, keepdims=False)
        came.append(lax.ppermute(block, "virt", [(i, (i + 2 * s) % n) for i in range(n)]))
    for block in came:
        reduced = reduced + block
    route = [(i * g + q, ((i + half) % n) * g + (q + g // 2) % g) for i in range(n) for q in range(g)]
    turned = lax.ppermute(reduced, ("virt", "pair"), route)
    return finish(mirror_row.reshape(1, -1), reduced, turned).T


def solution(mesh):
    in_specs = (P("pair", "virt"), P("virt", None), P("virt", None), P("pair"))
    out_specs = P("pair", "virt")
    return jax.shard_map(shards, mesh=mesh, in_specs=in_specs, out_specs=out_specs, check_vma=False)
```

time: 78.9 us -> 25.8 us (0.33)
  waiting for transfers between devices: 42.1 us -> 5.3 us
  between operations: 13.4 us -> 0.05 us
  matrix products: 8.29 us -> 0 us
  starting transfers between devices: 3.87 us -> 10.4 us
  Pallas kernels: 0 us -> 5 us
  local copies, waits for them, and re-layouts: 8.72 us -> 4.72 us
  other arithmetic: 2.27 us -> 0.04 us
    reduce_scatter x1 -> x0, waiting for transfers between devices: 36.7 us -> none  [shards(): lax.psum_scatter(partial_value, 'virt', scatter_dimension=1, tiled=True)]
    dot_general x1 -> x0, matrix products: 8.29 us -> none  [product(): jnp.dot(left_side, right_side, precision=lax.Precision.HIGHEST, preferred...]
    mul x2 -> x0, local copies, waits for them, and re-layouts: 7.72 us -> none  [shards(): integrals.reshape(tile_rows, TILE, col_tiles, TILE)]
    ppermute x2 -> x5, starting transfers between devices: 3.87 us -> 10.4 us  [the longest x3 5.86 us: shards(): lax.ppermute(block, 'virt', [(i, (i + 2 * s) % n) for i in range(n)])]
    pallas_call x0 -> x2, Pallas kernels: none -> 5 us  [the longest x1 3.43 us: ladder(): pl.pallas_call(functools.partial(ladder_kernel, parts), out_shape=jax.Sha...]
    unnamed x4 -> x10, local copies, waits for them, and re-layouts: 0.01 us -> 4.68 us
    add x1 -> x2, other arithmetic: 1.43 us -> 0.04 us  [the longest x1 0.03 us: shards(): mine = both[0] + arrived]
    convert_element_type x1 -> x0, other arithmetic: 0.82 us -> none  [shards(): tile_mask.astype(jnp.float32)[:, None, :, None]]
  transfers between devices with their start and end apart: 3 -> 5, of which waited for: 3 -> 5; matrix products, arithmetic and copies ran while one was open for 0% -> 0% of each run, Pallas kernels for 0% -> 0%
where the time goes in v1:
time: 25.8 us; the launch traced here: 25.5 us
  starting transfers between devices  10.4 us (40%)
  waiting for transfers between devices  5.3 us (21%)
  Pallas kernels  5 us (19%)
  local copies, waits for them, and re-layouts  4.72 us (18%)
    ppermute x3, starting transfers between devices, shards(): lax.ppermute(block, 'virt', [(i, (i + 2 * s) % n) for i in range(n)])  5.86 us
    unnamed x10, local copies, waits for them, and re-layouts  4.68 us
    ppermute x1, starting transfers between devices, shards(): turned = lax.ppermute(reduced, ('virt', 'pair'), route)  4.02 us
    pallas_call x1, Pallas kernels, ladder(): pl.pallas_call(functools.partial(ladder_kernel, parts), out_shape=jax.Sha...  3.43 us
    ppermute x3, waiting for transfers between devices, shards(): lax.ppermute(block, 'virt', [(i, (i + 2 * s) % n) for i in range(n)])  2.16 us
    ppermute x1, waiting for transfers between devices, shards(): turned = lax.ppermute(reduced, ('virt', 'pair'), route)  2.07 us
    pallas_call x1, Pallas kernels, finish(): pl.pallas_call(finish_kernel, out_shape=jax.ShapeDtypeStruct(own.shape, o...  1.57 us
    ppermute x1, waiting for transfers between devices, shards(): arrived = lax.ppermute(both[1], 'virt', [(i, i ^ 1) for i in range(n)])  1.07 us
  transfers between devices with their start and end apart: 5, of which 5 were waited for; matrix products, arithmetic and copies ran while one was open for 0% of the time, Pallas kernels for 0%

profile of v1, /device:TPU:0, one launch (start us, length us, event | category | flops | bytes accessed | tf_op | source)
XLA Modules:
  0.0 25.5 jit_solution(16122193763651385041)
XLA Ops:
  0.0 0.0 copy-start
  0.0 1.8 %copy-done = f32[1920,384]{1,0:T(8,128)S(1)} copy-done((f32[1920,384]{1,0:T(8,128)S(1)}, f32[1920,384]{1,0:T(8,128)}, u32[]{:S(2)}) %copy-start) | copy-done | bytes 2949144
  1.8 0.0 copy-start.1
  1.8 1.5 %copy-done.1 = f32[256,1920]{1,0:T(8,128)S(1)} copy-done((f32[256,1920]{1,0:T(8,128)S(1)}, f32[256,1920]{1,0:T(8,128)}, u32[]{:S(2)}) %copy-start.1) | copy-done | bytes 1966104
  3.4 0.0 copy-start.2
  3.4 0.7 %copy-done.2 = s32[20,4]{0,1:T(4,128)S(1)} copy-done((s32[20,4]{0,1:T(4,128)S(1)}, s32[20,4]{0,1:T(4,128)}, u32[]{:S(2)}) %copy-start.2) | copy-done | bytes 344
  4.1 3.4 %ladder.1 = f32[2,4,48,256]{3,2,1,0:T(8,128)S(1)} custom-call(s32[4,20]{1,0:T(4,128)S(1)} %bitcast.22, s32[1]{0:T(128)} %bitcast.2.side_ref, f32[256,1920]{1,0:T(8,128)S(1)} %copy-done.1, f32[1920,384]{1,0:T(8,128)S(1)} %copy-done), custom_call_target="tpu_custom_call" | custom-call | tf_op jit(solution)/shard_map/ladder/pallas_call | solution.py:69
  7.5 0.5 %collective-permute-start = (f32[4,48,256]{2,1,0:T(8,128)S(1)}, f32[4,48,256]{2,1,0:T(8,128)S(1)}, u32[]{:S(2)}, u32[]{:S(2)}) collective-permute-start(f32[4,48,256]{2,1,0:T(8,128)S(1)} %slice_bitcast_fusion), channel_id=1, source_target_pairs={{0,4},{4,0},{8,12},{12,8},{16,20},{20,16},{24,28},{28,24},{1,5},{5... | collective-permute-start | bytes 589832 | tf_op jit(solution)/shard_map/ppermute | solution.py:113
  8.0 1.1 %collective-permute-done = f32[4,48,256]{2,1,0:T(8,128)S(1)} collective-permute-done((f32[4,48,256]{2,1,0:T(8,128)S(1)}, f32[4,48,256]{2,1,0:T(8,128)S(1)}, u32[]{:S(2)}, u32[]{:S(2)}) %collective-permute-start) | collective-permute-done | bytes 196640 | tf_op jit(solution)/shard_map/ppermute | solution.py:113
  9.2 2.9 %collective-permute-start.1 = (f32[48,256]{1,0:T(8,128)S(1)}, f32[48,256]{1,0:T(8,128)S(1)}, u32[]{:S(2)}, u32[]{:S(2)}) collective-permute-start(f32[48,256]{1,0:T(8,128)S(1)} %get-tuple-element.5), channel_id=1, source_target_pairs={{0,8},{4,12},{8,16},{12,20},{16,24},{20,28},{24,0},{28,4},{1,9},{5... | collective-permute-start | bytes 147464 | tf_op jit(solution)/shard_map/ppermute | solution.py:119
  12.1 1.0 %collective-permute-start.3 = (f32[48,256]{1,0:T(8,128)S(1)}, f32[48,256]{1,0:T(8,128)S(1)}, u32[]{:S(2)}, u32[]{:S(2)}) collective-permute-start(f32[48,256]{1,0:T(8,128)S(1)} %get-tuple-element.6), channel_id=1, source_target_pairs={{0,24},{4,28},{8,0},{12,4},{16,8},{20,12},{24,16},{28,20},{1,25},{... | collective-permute-start | bytes 147464 | tf_op jit(solution)/shard_map/ppermute | solution.py:119
  13.1 1.9 %collective-permute-start.2 = (f32[48,256]{1,0:T(8,128)S(1)}, f32[48,256]{1,0:T(8,128)S(1)}, u32[]{:S(2)}, u32[]{:S(2)}) collective-permute-start(f32[48,256]{1,0:T(8,128)S(1)} %get-tuple-element.7), channel_id=1, source_target_pairs={{0,16},{4,20},{8,24},{12,28},{16,0},{20,4},{24,8},{28,12},{1,17},{... | collective-permute-start | bytes 147464 | tf_op jit(solution)/shard_map/ppermute | solution.py:119
  15.0 0.1 collective-permute-done.1
  15.1 1.3 %collective-permute-done.3 = f32[48,256]{1,0:T(8,128)S(1)} collective-permute-done((f32[48,256]{1,0:T(8,128)S(1)}, f32[48,256]{1,0:T(8,128)S(1)}, u32[]{:S(2)}, u32[]{:S(2)}) %collective-permute-start.3) | collective-permute-done | bytes 49184 | tf_op jit(solution)/shard_map/ppermute | solution.py:119
  16.4 0.8 %collective-permute-done.2 = f32[48,256]{1,0:T(8,128)S(1)} collective-permute-done((f32[48,256]{1,0:T(8,128)S(1)}, f32[48,256]{1,0:T(8,128)S(1)}, u32[]{:S(2)}, u32[]{:S(2)}) %collective-permute-start.2) | collective-permute-done | bytes 49184 | tf_op jit(solution)/shard_map/ppermute | solution.py:119
  17.2 0.0 copy-start.3
  17.2 4.0 %collective-permute-start.4 = (f32[48,256]{1,0:T(8,128)S(1)}, f32[48,256]{1,0:T(8,128)S(1)}, u32[]{:S(2)}, u32[]{:S(2)}) collective-permute-start(f32[48,256]{1,0:T(8,128)S(1)} %fusion.2.own_ref), channel_id=1, source_target_pairs={{0,18},{1,19},{2,16},{3,17},{4,22},{5,23},{6,20},{7,21},{8,26},{9,... | collective-permute-start | bytes 147464 | tf_op jit(solution)/shard_map/ppermute | solution.py:123
  21.2 2.1 %collective-permute-done.4.other_ref = f32[48,256]{1,0:T(8,128)S(1)} collective-permute-done((f32[48,256]{1,0:T(8,128)S(1)}, f32[48,256]{1,0:T(8,128)S(1)}, u32[]{:S(2)}, u32[]{:S(2)}) %collective-permute-start.4) | collective-permute-done | bytes 49184 | tf_op jit(solution)/shard_map/ppermute | solution.py:123
  23.3 0.0 copy-start.4
  23.3 0.0 copy-done.3
  23.3 0.6 %copy-done.4 = f32[48,256]{1,0:T(8,128)} copy-done((f32[48,256]{1,0:T(8,128)}, f32[48,256]{1,0:T(8,128)S(1)}, u32[]{:S(2)}) %copy-start.4) | copy-done | bytes 49176
  23.9 1.6 %finish.1 = f32[48,256]{1,0:T(8,128)} custom-call(s32[1,256]{1,0:T(1,128)} %bitcast.23, f32[48,256]{1,0:T(8,128)} %copy-done.3, f32[48,256]{1,0:T(8,128)} %copy-done.4), custom_call_target="tpu_custom_call" | custom-call | tf_op jit(solution)/shard_map/finish/pallas_call | solution.py:98
  (4 shorter events, 0.1 us)
Async XLA Ops:
  0.0 1.8 %copy-start = (f32[1920,384]{1,0:T(8,128)S(1)}, f32[1920,384]{1,0:T(8,128)}, u32[]{:S(2)}) copy-start(f32[1920,384]{1,0:T(8,128)} %int_ref.1) | copy-start | bytes 8847364
  1.8 1.5 %copy-start.1 = (f32[256,1920]{1,0:T(8,128)S(1)}, f32[256,1920]{1,0:T(8,128)}, u32[]{:S(2)}) copy-start(f32[256,1920]{1,0:T(8,128)} %amp_ref.1) | copy-start | bytes 5898244
  3.4 0.7 %copy-start.2 = (s32[20,4]{0,1:T(4,128)S(1)}, s32[20,4]{0,1:T(4,128)}, u32[]{:S(2)}) copy-start(s32[20,4]{0,1:T(4,128)} %param.6) | copy-start | bytes 964
  7.5 1.6 %collective-permute-start = (f32[4,48,256]{2,1,0:T(8,128)S(1)}, f32[4,48,256]{2,1,0:T(8,128)S(1)}, u32[]{:S(2)}, u32[]{:S(2)}) collective-permute-start(f32[4,48,256]{2,1,0:T(8,128)S(1)} %slice_bitcast_fusion), channel_id=1, source_target_pairs={{0,4},{4,0},{8,12},{12,8},{16,20},{20,16},{24,28},{28,24},{1,5},{5... | collective-permute-start | bytes 589832 | tf_op jit(solution)/shard_map/ppermute | solution.py:113
  9.2 5.9 %collective-permute-start.1 = (f32[48,256]{1,0:T(8,128)S(1)}, f32[48,256]{1,0:T(8,128)S(1)}, u32[]{:S(2)}, u32[]{:S(2)}) collective-permute-start(f32[48,256]{1,0:T(8,128)S(1)} %get-tuple-element.5), channel_id=1, source_target_pairs={{0,8},{4,12},{8,16},{12,20},{16,24},{20,28},{24,0},{28,4},{1,9},{5... | collective-permute-start | bytes 147464 | tf_op jit(solution)/shard_map/ppermute | solution.py:119
  12.1 4.3 %collective-permute-start.3 = (f32[48,256]{1,0:T(8,128)S(1)}, f32[48,256]{1,0:T(8,128)S(1)}, u32[]{:S(2)}, u32[]{:S(2)}) collective-permute-start(f32[48,256]{1,0:T(8,128)S(1)} %get-tuple-element.6), channel_id=1, source_target_pairs={{0,24},{4,28},{8,0},{12,4},{16,8},{20,12},{24,16},{28,20},{1,25},{... | collective-permute-start | bytes 147464 | tf_op jit(solution)/shard_map/ppermute | solution.py:119
  13.1 4.1 %collective-permute-start.2 = (f32[48,256]{1,0:T(8,128)S(1)}, f32[48,256]{1,0:T(8,128)S(1)}, u32[]{:S(2)}, u32[]{:S(2)}) collective-permute-start(f32[48,256]{1,0:T(8,128)S(1)} %get-tuple-element.7), channel_id=1, source_target_pairs={{0,16},{4,20},{8,24},{12,28},{16,0},{20,4},{24,8},{28,12},{1,17},{... | collective-permute-start | bytes 147464 | tf_op jit(solution)/shard_map/ppermute | solution.py:119
  17.2 6.1 %copy-start.3 = (f32[48,256]{1,0:T(8,128)}, f32[48,256]{1,0:T(8,128)S(1)}, u32[]{:S(2)}) copy-start(f32[48,256]{1,0:T(8,128)S(1)} %fusion.2.own_ref) | copy-start | bytes 147460
  17.2 6.1 %collective-permute-start.4 = (f32[48,256]{1,0:T(8,128)S(1)}, f32[48,256]{1,0:T(8,128)S(1)}, u32[]{:S(2)}, u32[]{:S(2)}) collective-permute-start(f32[48,256]{1,0:T(8,128)S(1)} %fusion.2.own_ref), channel_id=1, source_target_pairs={{0,18},{1,19},{2,16},{3,17},{4,22},{5,23},{6,20},{7,21},{8,26},{9,... | collective-permute-start | bytes 147464 | tf_op jit(solution)/shard_map/ppermute | solution.py:123
  23.3 0.6 %copy-start.4 = (f32[48,256]{1,0:T(8,128)}, f32[48,256]{1,0:T(8,128)S(1)}, u32[]{:S(2)}) copy-start(f32[48,256]{1,0:T(8,128)S(1)} %collective-permute-done.4.other_ref) | copy-start | bytes 147460

commit v2 on v1

--- a/solution.py
+++ b/solution.py
@@ -21,10 +21,13 @@
     return [(start, min(CHUNK, extent - start)) for start in range(0, extent, CHUNK)]
 
 
-def ladder_kernel(parts, mask_ref, side_ref, amp_ref, int_ref, out_ref, amp, ints, sems):
+def ladder_kernel(parts, side_ref, mask_hbm, mirror_hbm, amp_ref, int_ref, out_ref, mirror_out, mask_ref, amp, ints, sems, sem2):
     depth, cols = int_ref.shape
     rows = amp_ref.shape[0]
     spans = chunks_of(depth)
+    small = [pltpu.make_async_copy(mask_hbm, mask_ref, sem2.at[0]), pltpu.make_async_copy(mirror_hbm, mirror_out, sem2.at[1])]
+    for copy in small:
+        copy.start()
     copies = []
     for i, (start, size) in enumerate(spans):
         span = pl.ds(start, size)
@@ -38,6 +41,8 @@
     tile_r, tile_c = depth // tile_rows, cols // col_tiles
     lane = lax.broadcasted_iota(jnp.int32, (1, cols), 1)
     total = jnp.zeros((rows, cols), jnp.float32)
+    for copy in small:
+        copy.wait()
     for (start, size), (one, two) in zip(spans, copies):
         one.wait()
         two.wait()
@@ -62,23 +67,28 @@
         out_ref[(b % 2) ^ side_ref[0], b // 2] = turned[b * block:(b + 1) * block, :]
 
 
-def ladder(parts, mask, side, amplitudes, integrals):
+def ladder(parts, side, mask, mirror, amplitudes, integrals):
     rows, depth = amplitudes.shape
     cols = integrals.shape[1]
     count = len(chunks_of(depth))
     return pl.pallas_call(
         functools.partial(ladder_kernel, parts),
-        out_shape=jax.ShapeDtypeStruct((2, parts // 2, cols // parts, rows), jnp.float32),
-        in_specs=[pl.BlockSpec(memory_space=pltpu.SMEM)] * 2 + [pl.BlockSpec(memory_space=pl.ANY)] * 2,
-        out_specs=pl.BlockSpec(memory_space=pltpu.VMEM),
+        out_shape=(
+            jax.ShapeDtypeStruct((2, parts // 2, cols // parts, rows), jnp.float32),
+            jax.ShapeDtypeStruct(mirror.shape, mirror.dtype),
+        ),
+        in_specs=[pl.BlockSpec(memory_space=pltpu.SMEM)] + [pl.BlockSpec(memory_space=pltpu.HBM)] * 4,
+        out_specs=(pl.BlockSpec(memory_space=pltpu.VMEM),) * 2,
         scratch_shapes=[
+            pltpu.SMEM(mask.shape, mask.dtype),
             pltpu.VMEM((rows, depth), jnp.float32),
             pltpu.VMEM((depth, cols), jnp.float32),
             pltpu.SemaphoreType.DMA((2, count)),
+            pltpu.SemaphoreType.DMA((2,)),
         ],
-        compiler_params=pltpu.CompilerParams(vmem_limit_bytes=40 * MIB),
+        compiler_params=pltpu.CompilerParams(vmem_limit_bytes=16 * MIB),
         name="ladder",
-    )(mask, side, amplitudes, integrals)
+    )(side, *(pltpu.with_memory_space_constraint(x, pltpu.HBM) for x in (mask, mirror, amplitudes, integrals)))
 
 
 def finish_kernel(mirror_ref, own_ref, other_ref, out_ref):
@@ -100,6 +110,7 @@
         out_shape=jax.ShapeDtypeStruct(own.shape, own.dtype),
         in_specs=[pl.BlockSpec(memory_space=pltpu.VMEM)] * 3,
         out_specs=pl.BlockSpec(memory_space=pltpu.VMEM),
+        compiler_params=pltpu.CompilerParams(vmem_limit_bytes=4 * MIB),
         name="finish",
     )(mirror, own, other)
 
@@ -109,7 +120,7 @@
     v = lax.axis_index("virt")
     side, chip = v % 2, v // 2
     half = n // 2
-    both = ladder(n, tile_mask.T, side.reshape(1), amplitudes, integrals)
+    both, mirror = ladder(n, side.reshape(1), tile_mask.T, mirror_row.reshape(1, -1), amplitudes, integrals)
     arrived = lax.ppermute(both[1], "virt", [(i, i ^ 1) for i in range(n)])
     mine = both[0] + arrived
     reduced = lax.dynamic_index_in_dim(mine, chip, 0, keepdims=False)
@@ -121,7 +132,7 @@
         reduced = reduced + block
     route = [(i * g + q, ((i + half) % n) * g + (q + g // 2) % g) for i in range(n) for q in range(g)]
     turned = lax.ppermute(reduced, ("virt", "pair"), route)
-    return finish(mirror_row.reshape(1, -1), reduced, turned).T
+    return finish(mirror, reduced, turned).T
 
 
 def solution(mesh):

time: 25.8 us -> 21.1 us (0.82)
  local copies, waits for them, and re-layouts: 4.72 us -> 0.04 us
    unnamed x10 -> x0, local copies, waits for them, and re-layouts: 4.68 us -> none
    pallas_call x1, Pallas kernels: 3.43 us -> 4.45 us  [ladder(): pl.pallas_call(functools.partial(ladder_kernel, parts), out_shape=(jax.Sh...]
    pallas_call x1, Pallas kernels: 1.57 us -> 0.73 us  [finish(): pl.pallas_call(finish_kernel, out_shape=jax.ShapeDtypeStruct(own.shape, o...]
where the time goes in v2:
time: 21.1 us; the launch traced here: 21 us
  starting transfers between devices  10.4 us (49%)
  waiting for transfers between devices  5.3 us (25%)
  Pallas kernels  5.18 us (25%)
    ppermute x3, starting transfers between devices, shards(): lax.ppermute(block, 'virt', [(i, (i + 2 * s) % n) for i in range(n)])  5.86 us
    pallas_call x1, Pallas kernels, ladder(): pl.pallas_call(functools.partial(ladder_kernel, parts), out_shape=(jax.Sh...  4.45 us
    ppermute x1, starting transfers between devices, shards(): turned = lax.ppermute(reduced, ('virt', 'pair'), route)  4.02 us
    ppermute x3, waiting for transfers between devices, shards(): lax.ppermute(block, 'virt', [(i, (i + 2 * s) % n) for i in range(n)])  2.16 us
    ppermute x1, waiting for transfers between devices, shards(): turned = lax.ppermute(reduced, ('virt', 'pair'), route)  2.07 us
    ppermute x1, waiting for transfers between devices, shards(): arrived = lax.ppermute(both[1], 'virt', [(i, i ^ 1) for i in range(n)])  1.07 us
    pallas_call x1, Pallas kernels, finish(): pl.pallas_call(finish_kernel, out_shape=jax.ShapeDtypeStruct(own.shape, o...  0.73 us
    ppermute x1, starting transfers between devices, shards(): arrived = lax.ppermute(both[1], 'virt', [(i, i ^ 1) for i in range(n)])  0.52 us
  transfers between devices with their start and end apart: 5, of which 5 were waited for; matrix products, arithmetic and copies ran while one was open for 0% of the time, Pallas kernels for 0%

profile of v2, /device:TPU:0, one launch (start us, length us, event | category | flops | bytes accessed | tf_op | source)
XLA Modules:
  0.0 21.0 jit_solution(9259360714531144909)
XLA Ops:
  0.0 4.5 %ladder.1 = (f32[2,4,48,256]{3,2,1,0:T(8,128)S(1)}, s32[1,256]{1,0:T(1,128)S(1)}) custom-call(s32[1]{0:T(128)} %bitcast.side_ref, s32[4,20]{1,0:T(4,128)} %bitcast.20, s32[1,256]{1,0:T(1,128)} %bitcast.21, f32[256,1920]{1,0:T(8,128)} %amp_ref.1, f32[1920,384]{1,0:T(8,128)} %int_ref.1), custom_call_target="tpu_custom_call" | custom-call | tf_op jit(solution)/shard_map/ladder/pallas_call | solution.py:74
  4.5 0.5 %collective-permute-start = (f32[4,48,256]{2,1,0:T(8,128)S(1)}, f32[4,48,256]{2,1,0:T(8,128)S(1)}, u32[]{:S(2)}, u32[]{:S(2)}) collective-permute-start(f32[4,48,256]{2,1,0:T(8,128)S(1)} %slice_bitcast_fusion), channel_id=1, source_target_pairs={{0,4},{4,0},{8,12},{12,8},{16,20},{20,16},{24,28},{28,24},{1,5},{5... | collective-permute-start | bytes 589832 | tf_op jit(solution)/shard_map/ppermute | solution.py:124
  5.0 1.1 %collective-permute-done = f32[4,48,256]{2,1,0:T(8,128)S(1)} collective-permute-done((f32[4,48,256]{2,1,0:T(8,128)S(1)}, f32[4,48,256]{2,1,0:T(8,128)S(1)}, u32[]{:S(2)}, u32[]{:S(2)}) %collective-permute-start) | collective-permute-done | bytes 196640 | tf_op jit(solution)/shard_map/ppermute | solution.py:124
  6.1 2.9 %collective-permute-start.1 = (f32[48,256]{1,0:T(8,128)S(1)}, f32[48,256]{1,0:T(8,128)S(1)}, u32[]{:S(2)}, u32[]{:S(2)}) collective-permute-start(f32[48,256]{1,0:T(8,128)S(1)} %get-tuple-element.9), channel_id=1, source_target_pairs={{0,8},{4,12},{8,16},{12,20},{16,24},{20,28},{24,0},{28,4},{1,9},{5... | collective-permute-start | bytes 147464 | tf_op jit(solution)/shard_map/ppermute | solution.py:130
  9.0 1.0 %collective-permute-start.3 = (f32[48,256]{1,0:T(8,128)S(1)}, f32[48,256]{1,0:T(8,128)S(1)}, u32[]{:S(2)}, u32[]{:S(2)}) collective-permute-start(f32[48,256]{1,0:T(8,128)S(1)} %get-tuple-element.10), channel_id=1, source_target_pairs={{0,24},{4,28},{8,0},{12,4},{16,8},{20,12},{24,16},{28,20},{1,25},{... | collective-permute-start | bytes 147464 | tf_op jit(solution)/shard_map/ppermute | solution.py:130
  10.1 1.9 %collective-permute-start.2 = (f32[48,256]{1,0:T(8,128)S(1)}, f32[48,256]{1,0:T(8,128)S(1)}, u32[]{:S(2)}, u32[]{:S(2)}) collective-permute-start(f32[48,256]{1,0:T(8,128)S(1)} %get-tuple-element.11), channel_id=1, source_target_pairs={{0,16},{4,20},{8,24},{12,28},{16,0},{20,4},{24,8},{28,12},{1,17},{... | collective-permute-start | bytes 147464 | tf_op jit(solution)/shard_map/ppermute | solution.py:130
  12.0 0.1 collective-permute-done.1
  12.1 1.3 %collective-permute-done.3 = f32[48,256]{1,0:T(8,128)S(1)} collective-permute-done((f32[48,256]{1,0:T(8,128)S(1)}, f32[48,256]{1,0:T(8,128)S(1)}, u32[]{:S(2)}, u32[]{:S(2)}) %collective-permute-start.3) | collective-permute-done | bytes 49184 | tf_op jit(solution)/shard_map/ppermute | solution.py:130
  13.3 0.8 %collective-permute-done.2 = f32[48,256]{1,0:T(8,128)S(1)} collective-permute-done((f32[48,256]{1,0:T(8,128)S(1)}, f32[48,256]{1,0:T(8,128)S(1)}, u32[]{:S(2)}, u32[]{:S(2)}) %collective-permute-start.2) | collective-permute-done | bytes 49184 | tf_op jit(solution)/shard_map/ppermute | solution.py:130
  14.2 4.0 %collective-permute-start.4 = (f32[48,256]{1,0:T(8,128)S(1)}, f32[48,256]{1,0:T(8,128)S(1)}, u32[]{:S(2)}, u32[]{:S(2)}) collective-permute-start(f32[48,256]{1,0:T(8,128)S(1)} %fusion.1.own_ref), channel_id=1, source_target_pairs={{0,18},{1,19},{2,16},{3,17},{4,22},{5,23},{6,20},{7,21},{8,26},{9,... | collective-permute-start | bytes 147464 | tf_op jit(solution)/shard_map/ppermute | solution.py:134
  18.2 2.1 %collective-permute-done.4.other_ref = f32[48,256]{1,0:T(8,128)S(1)} collective-permute-done((f32[48,256]{1,0:T(8,128)S(1)}, f32[48,256]{1,0:T(8,128)S(1)}, u32[]{:S(2)}, u32[]{:S(2)}) %collective-permute-start.4) | collective-permute-done | bytes 49184 | tf_op jit(solution)/shard_map/ppermute | solution.py:134
  20.3 0.7 %finish.1 = f32[48,256]{1,0:T(8,128)} custom-call(s32[1,256]{1,0:T(1,128)S(1)} %get-tuple-element.7.mirror_ref, f32[48,256]{1,0:T(8,128)S(1)} %fusion.1.own_ref, f32[48,256]{1,0:T(8,128)S(1)} %collective-permute-done.4.other_ref), custom_call_target="tpu_custom_call" | custom-call | tf_op jit(solution)/shard_map/finish/pallas_call | solution.py:108
  (4 shorter events, 0.1 us)
Async XLA Ops:
  4.5 1.6 %collective-permute-start = (f32[4,48,256]{2,1,0:T(8,128)S(1)}, f32[4,48,256]{2,1,0:T(8,128)S(1)}, u32[]{:S(2)}, u32[]{:S(2)}) collective-permute-start(f32[4,48,256]{2,1,0:T(8,128)S(1)} %slice_bitcast_fusion), channel_id=1, source_target_pairs={{0,4},{4,0},{8,12},{12,8},{16,20},{20,16},{24,28},{28,24},{1,5},{5... | collective-permute-start | bytes 589832 | tf_op jit(solution)/shard_map/ppermute | solution.py:124
  6.1 5.9 %collective-permute-start.1 = (f32[48,256]{1,0:T(8,128)S(1)}, f32[48,256]{1,0:T(8,128)S(1)}, u32[]{:S(2)}, u32[]{:S(2)}) collective-permute-start(f32[48,256]{1,0:T(8,128)S(1)} %get-tuple-element.9), channel_id=1, source_target_pairs={{0,8},{4,12},{8,16},{12,20},{16,24},{20,28},{24,0},{28,4},{1,9},{5... | collective-permute-start | bytes 147464 | tf_op jit(solution)/shard_map/ppermute | solution.py:130
  9.0 4.3 %collective-permute-start.3 = (f32[48,256]{1,0:T(8,128)S(1)}, f32[48,256]{1,0:T(8,128)S(1)}, u32[]{:S(2)}, u32[]{:S(2)}) collective-permute-start(f32[48,256]{1,0:T(8,128)S(1)} %get-tuple-element.10), channel_id=1, source_target_pairs={{0,24},{4,28},{8,0},{12,4},{16,8},{20,12},{24,16},{28,20},{1,25},{... | collective-permute-start | bytes 147464 | tf_op jit(solution)/shard_map/ppermute | solution.py:130
  10.1 4.1 %collective-permute-start.2 = (f32[48,256]{1,0:T(8,128)S(1)}, f32[48,256]{1,0:T(8,128)S(1)}, u32[]{:S(2)}, u32[]{:S(2)}) collective-permute-start(f32[48,256]{1,0:T(8,128)S(1)} %get-tuple-element.11), channel_id=1, source_target_pairs={{0,16},{4,20},{8,24},{12,28},{16,0},{20,4},{24,8},{28,12},{1,17},{... | collective-permute-start | bytes 147464 | tf_op jit(solution)/shard_map/ppermute | solution.py:130
  14.2 6.1 %collective-permute-start.4 = (f32[48,256]{1,0:T(8,128)S(1)}, f32[48,256]{1,0:T(8,128)S(1)}, u32[]{:S(2)}, u32[]{:S(2)}) collective-permute-start(f32[48,256]{1,0:T(8,128)S(1)} %fusion.1.own_ref), channel_id=1, source_target_pairs={{0,18},{1,19},{2,16},{3,17},{4,22},{5,23},{6,20},{7,21},{8,26},{9,... | collective-permute-start | bytes 147464 | tf_op jit(solution)/shard_map/ppermute | solution.py:134

commit v3 on v1

v3 whole, which is shorter than its diff:
```python
import functools

import jax
import jax.numpy as jnp
from jax import lax
from jax.experimental import pallas as pl
from jax.experimental.pallas import tpu as pltpu
from jax.sharding import PartitionSpec as P

CHUNK = 512
MIB = 1 << 20


def split(x):
    high = x.astype(jnp.bfloat16)
    low = (x - high.astype(jnp.float32)).astype(jnp.bfloat16)
    return high, low


def chunks_of(extent):
    starts = list(range(0, max(extent - CHUNK, 1), CHUNK))
    return list(zip(starts, [b - a for a, b in zip(starts, starts[1:] + [extent])]))


def ladder_kernel(place, mask_hbm, amp_hbm, int_hbm, out_ref, mask_ref, amp, ints, sems, small_sem):
    depth, cols = int_hbm.shape
    rows = amp_hbm.shape[0]
    spans = chunks_of(depth)
    small = pltpu.make_async_copy(mask_hbm, mask_ref, small_sem)
    large = []
    for i, (start, size) in enumerate(spans):
        span = pl.ds(start, size)
        large.append((
            pltpu.make_async_copy(amp_hbm.at[:, span], amp.at[:, span], sems.at[0, i]),
            pltpu.make_async_copy(int_hbm.at[span, :], ints.at[span, :], sems.at[1, i]),
        ))
    small.start()
    for pair in large:
        for copy in pair:
            copy.start()

    col_tiles, tile_rows = mask_ref.shape
    tile_r, tile_c = depth // tile_rows, cols // col_tiles
    lane = lax.broadcasted_iota(jnp.int32, (1, cols), 1)
    total = jnp.zeros((rows, cols), jnp.float32)
    small.wait()
    dot = functools.partial(jnp.dot, preferred_element_type=jnp.float32)
    for (start, size), pair in zip(spans, large):
        for copy in pair:
            copy.wait()
        pieces = []
        at = start
        while at < start + size:
            t = at // tile_r
            end = min((t + 1) * tile_r, start + size)
            factor = jnp.full((1, cols), mask_ref[0, t].astype(jnp.float32))
            for u in range(1, col_tiles):
                factor = jnp.where(lane >= u * tile_c, mask_ref[u, t].astype(jnp.float32), factor)
            pieces.append(ints[at:end, :] * factor)
            at = end
        b_high, b_low = split(jnp.concatenate(pieces, axis=0))
        a_high, a_low = split(amp[:, start:start + size])
        wide = dot(a_high, jnp.concatenate([b_high, b_low], axis=1))
        total += wide[:, :cols] + wide[:, cols:] + dot(a_low, b_high)
    turned = total.T
    block = out_ref.shape[-2]
    for b in range(cols // block):
        where = place(b)
        out_ref[where] = turned[b * block:(b + 1) * block, :]


def ladder(parts, place, mask, amplitudes, integrals):
    rows, depth = amplitudes.shape
    cols = integrals.shape[1]
    count = len(chunks_of(depth))
    operands = [pltpu.with_memory_space_constraint(x, pltpu.HBM) for x in (mask, amplitudes, integrals)]
    return pl.pallas_call(
        functools.partial(ladder_kernel, place),
        out_shape=jax.ShapeDtypeStruct((2, parts // 2, cols // parts, rows), jnp.float32),
        in_specs=[pl.BlockSpec(memory_space=pltpu.HBM)] * 3,
        out_specs=pl.BlockSpec(memory_space=pltpu.VMEM),
        scratch_shapes=[
            pltpu.SMEM(mask.shape, mask.dtype),
            pltpu.VMEM((rows, depth), jnp.float32),
            pltpu.VMEM((depth, cols), jnp.float32),
            pltpu.SemaphoreType.DMA((2, count)),
            pltpu.SemaphoreType.DMA,
        ],
        compiler_params=pltpu.CompilerParams(vmem_limit_bytes=16 * MIB),
        name="ladder",
    )(*operands)


def finish_kernel(mirror_ref, own_ref, other_ref, out_ref):
    rows = own_ref.shape[1]
    lanes = 128
    for j in range(0, rows, lanes):
        index = jnp.broadcast_to(mirror_ref[:, j:j + lanes], (own_ref.shape[0], lanes))
        picked = own_ref[:, j:j + lanes]
        for k in range(0, rows, lanes):
            inside = (index >= k) & (index < k + lanes)
            found = jnp.take_along_axis(other_ref[:, k:k + lanes], jnp.where(inside, index - k, 0), axis=1)
            picked += jnp.where(inside, found, 0.0)
        out_ref[:, j:j + lanes] = picked


def finish(mirror, own, other):
    return pl.pallas_call(
        finish_kernel,
        out_shape=jax.ShapeDtypeStruct(own.shape, own.dtype),
        in_specs=[pl.BlockSpec(memory_space=pltpu.VMEM)] * 3,
        out_specs=pl.BlockSpec(memory_space=pltpu.VMEM),
        compiler_params=pltpu.CompilerParams(vmem_limit_bytes=4 * MIB),
        name="finish",
    )(mirror, own, other)


def shards(amplitudes, integrals, tile_mask, mirror_row):
    n, g = lax.axis_size("virt"), lax.axis_size("pair")
    chips = n // 2

    def place(b):
        v = lax.axis_index("virt")
        side, chip = lax.rem(v, 2), lax.div(v, 2)
        s = lax.rem(b // 2 - chip + chips, chips)
        sender = jnp.where(s == 0, b % 2, 1 - b % 2)
        return jnp.where(sender == side, 0, 1), s

    both = ladder(n, place, tile_mask.T, amplitudes, integrals)
    mine = both[0] + lax.ppermute(both[1], "virt", [(i, i ^ 1) for i in range(n)])
    reduced = mine[0]
    came = []
    for s in range(1, chips):
        came.append(lax.ppermute(mine[s], "virt", [(i, ((i + 2 * s) % n) ^ 1) for i in range(n)]))
    for block in came:
        reduced = reduced + block
    route = [(i * g + q, ((i + chips) % n) * g + (q + g // 2) % g) for i in range(n) for q in range(g)]
    turned = lax.ppermute(reduced, ("virt", "pair"), route)
    return finish(mirror_row.reshape(1, -1), reduced, turned).T


def solution(mesh):
    in_specs = (P("pair", "virt"), P("virt", None), P("virt", None), P("pair"))
    out_specs = P("pair", "virt")
    return jax.shard_map(shards, mesh=mesh, in_specs=in_specs, out_specs=out_specs, check_vma=False)
```

time: 25.8 us -> 19.5 us (0.76)
  local copies, waits for them, and re-layouts: 4.72 us -> 0.03 us
  Pallas kernels: 5 us -> 4.17 us
  starting transfers between devices: 10.4 us -> 10 us
  waiting for transfers between devices: 5.3 us -> 5.02 us
    unnamed x10 -> x2, local copies, waits for them, and re-layouts: 4.68 us -> 0.01 us
    pallas_call x1, Pallas kernels: 1.57 us -> 0.73 us  [finish(): pl.pallas_call(finish_kernel, out_shape=jax.ShapeDtypeStruct(own.shape, o...]
    ppermute x4, starting transfers between devices: 6.38 us -> 5.86 us  [the longest x3 5.34 us: shards(): lax.ppermute(mine[s], 'virt', [(i, (i + 2 * s) % n ^ 1) for i in range(n)])]
    ppermute x4, waiting for transfers between devices: 3.23 us -> 2.94 us  [the longest x3 1.87 us: shards(): lax.ppermute(mine[s], 'virt', [(i, (i + 2 * s) % n ^ 1) for i in range(n)])]
where the time goes in v3:
time: 19.5 us; the launch traced here: 19.3 us
  starting transfers between devices  10 us (51%)
  waiting for transfers between devices  5.02 us (26%)
  Pallas kernels  4.17 us (21%)
    ppermute x3, starting transfers between devices, shards(): lax.ppermute(mine[s], 'virt', [(i, (i + 2 * s) % n ^ 1) for i in range(n)])  5.34 us
    ppermute x1, starting transfers between devices, shards(): turned = lax.ppermute(reduced, ('virt', 'pair'), route)  4.17 us
    pallas_call x1, Pallas kernels, ladder(): pl.pallas_call(functools.partial(ladder_kernel, place), out_shape=jax.Sha...  3.44 us
    ppermute x1, waiting for transfers between devices, shards(): turned = lax.ppermute(reduced, ('virt', 'pair'), route)  2.08 us
    ppermute x3, waiting for transfers between devices, shards(): lax.ppermute(mine[s], 'virt', [(i, (i + 2 * s) % n ^ 1) for i in range(n)])  1.87 us
    ppermute x1, waiting for transfers between devices, shards(): lax.ppermute(both[1], 'virt', [(i, i ^ 1) for i in range(n)])  1.07 us
    pallas_call x1, Pallas kernels, finish(): pl.pallas_call(finish_kernel, out_shape=jax.ShapeDtypeStruct(own.shape, o...  0.73 us
    ppermute x1, starting transfers between devices, shards(): lax.ppermute(both[1], 'virt', [(i, i ^ 1) for i in range(n)])  0.52 us
  transfers between devices with their start and end apart: 5, of which 5 were waited for; matrix products, arithmetic and copies ran while one was open for 0% of the time, Pallas kernels for 0%

profile of v3, /device:TPU:0, one launch (start us, length us, event | category | flops | bytes accessed | tf_op | source)
XLA Modules:
  0.0 19.3 jit_solution(10059840897134335999)
XLA Ops:
  0.0 0.0 copy-start
  0.0 3.4 %ladder.1 = f32[2,4,48,256]{3,2,1,0:T(8,128)S(1)} custom-call(s32[4,20]{1,0:T(4,128)} %bitcast.24, f32[256,1920]{1,0:T(8,128)} %amp_hbm.1, f32[1920,384]{1,0:T(8,128)} %int_hbm.1), custom_call_target="tpu_custom_call" | custom-call | tf_op jit(solution)/shard_map/ladder/pallas_call | solution.py:77
  3.5 0.5 %collective-permute-start = (f32[4,48,256]{2,1,0:T(8,128)S(1)}, f32[4,48,256]{2,1,0:T(8,128)S(1)}, u32[]{:S(2)}, u32[]{:S(2)}) collective-permute-start(f32[4,48,256]{2,1,0:T(8,128)S(1)} %slice_bitcast_fusion), channel_id=1, source_target_pairs={{0,4},{4,0},{8,12},{12,8},{16,20},{20,16},{24,28},{28,24},{1,5},{5... | collective-permute-start | bytes 589832 | tf_op jit(solution)/shard_map/ppermute | solution.py:130
  4.0 1.1 %collective-permute-done = f32[4,48,256]{2,1,0:T(8,128)S(1)} collective-permute-done((f32[4,48,256]{2,1,0:T(8,128)S(1)}, f32[4,48,256]{2,1,0:T(8,128)S(1)}, u32[]{:S(2)}, u32[]{:S(2)}) %collective-permute-start) | collective-permute-done | bytes 196640 | tf_op jit(solution)/shard_map/ppermute | solution.py:130
  5.1 2.7 %collective-permute-start.1 = (f32[48,256]{1,0:T(8,128)S(1)}, f32[48,256]{1,0:T(8,128)S(1)}, u32[]{:S(2)}, u32[]{:S(2)}) collective-permute-start(f32[48,256]{1,0:T(8,128)S(1)} %get-tuple-element.5), channel_id=1, source_target_pairs={{0,12},{4,8},{8,20},{12,16},{16,28},{20,24},{24,4},{28,0},{1,13},{... | collective-permute-start | bytes 147464 | tf_op jit(solution)/shard_map/ppermute | solution.py:134
  7.8 1.0 %collective-permute-start.3 = (f32[48,256]{1,0:T(8,128)S(1)}, f32[48,256]{1,0:T(8,128)S(1)}, u32[]{:S(2)}, u32[]{:S(2)}) collective-permute-start(f32[48,256]{1,0:T(8,128)S(1)} %get-tuple-element.6), channel_id=1, source_target_pairs={{0,28},{4,24},{8,4},{12,0},{16,12},{20,8},{24,20},{28,16},{1,29},{... | collective-permute-start | bytes 147464 | tf_op jit(solution)/shard_map/ppermute | solution.py:134
  8.8 1.7 %collective-permute-start.2 = (f32[48,256]{1,0:T(8,128)S(1)}, f32[48,256]{1,0:T(8,128)S(1)}, u32[]{:S(2)}, u32[]{:S(2)}) collective-permute-start(f32[48,256]{1,0:T(8,128)S(1)} %get-tuple-element.7), channel_id=1, source_target_pairs={{0,20},{4,16},{8,28},{12,24},{16,4},{20,0},{24,12},{28,8},{1,21},{... | collective-permute-start | bytes 147464 | tf_op jit(solution)/shard_map/ppermute | solution.py:134
  10.5 0.1 collective-permute-done.1
  10.5 1.8 %collective-permute-done.3 = f32[48,256]{1,0:T(8,128)S(1)} collective-permute-done((f32[48,256]{1,0:T(8,128)S(1)}, f32[48,256]{1,0:T(8,128)S(1)}, u32[]{:S(2)}, u32[]{:S(2)}) %collective-permute-start.3) | collective-permute-done | bytes 49184 | tf_op jit(solution)/shard_map/ppermute | solution.py:134
  12.3 0.1 collective-permute-done.2
  12.3 4.2 %collective-permute-start.4 = (f32[48,256]{1,0:T(8,128)S(1)}, f32[48,256]{1,0:T(8,128)S(1)}, u32[]{:S(2)}, u32[]{:S(2)}) collective-permute-start(f32[48,256]{1,0:T(8,128)S(1)} %fusion.3.own_ref), channel_id=1, source_target_pairs={{0,18},{1,19},{2,16},{3,17},{4,22},{5,23},{6,20},{7,21},{8,26},{9,... | collective-permute-start | bytes 147464 | tf_op jit(solution)/shard_map/ppermute | solution.py:138
  16.5 2.1 %collective-permute-done.4.other_ref = f32[48,256]{1,0:T(8,128)S(1)} collective-permute-done((f32[48,256]{1,0:T(8,128)S(1)}, f32[48,256]{1,0:T(8,128)S(1)}, u32[]{:S(2)}, u32[]{:S(2)}) %collective-permute-start.4) | collective-permute-done | bytes 49184 | tf_op jit(solution)/shard_map/ppermute | solution.py:138
  18.6 0.0 copy-done
  18.6 0.7 %finish.1 = f32[48,256]{1,0:T(8,128)} custom-call(s32[1,256]{1,0:T(1,128)S(1)} %bitcast.23, f32[48,256]{1,0:T(8,128)S(1)} %fusion.3.own_ref, f32[48,256]{1,0:T(8,128)S(1)} %collective-permute-done.4.other_ref), custom_call_target="tpu_custom_call" | custom-call | tf_op jit(solution)/shard_map/finish/pallas_call | solution.py:108
  (4 shorter events, 0.1 us)
Async XLA Ops:
  0.0 18.6 %copy-start = (s32[256]{0:T(256)S(1)}, s32[256]{0:T(256)}, u32[]{:S(2)}) copy-start(s32[256]{0:T(256)} %param.7) | copy-start | bytes 3076
  3.5 1.6 %collective-permute-start = (f32[4,48,256]{2,1,0:T(8,128)S(1)}, f32[4,48,256]{2,1,0:T(8,128)S(1)}, u32[]{:S(2)}, u32[]{:S(2)}) collective-permute-start(f32[4,48,256]{2,1,0:T(8,128)S(1)} %slice_bitcast_fusion), channel_id=1, source_target_pairs={{0,4},{4,0},{8,12},{12,8},{16,20},{20,16},{24,28},{28,24},{1,5},{5... | collective-permute-start | bytes 589832 | tf_op jit(solution)/shard_map/ppermute | solution.py:130
  5.1 5.4 %collective-permute-start.1 = (f32[48,256]{1,0:T(8,128)S(1)}, f32[48,256]{1,0:T(8,128)S(1)}, u32[]{:S(2)}, u32[]{:S(2)}) collective-permute-start(f32[48,256]{1,0:T(8,128)S(1)} %get-tuple-element.5), channel_id=1, source_target_pairs={{0,12},{4,8},{8,20},{12,16},{16,28},{20,24},{24,4},{28,0},{1,13},{... | collective-permute-start | bytes 147464 | tf_op jit(solution)/shard_map/ppermute | solution.py:134
  7.8 4.5 %collective-permute-start.3 = (f32[48,256]{1,0:T(8,128)S(1)}, f32[48,256]{1,0:T(8,128)S(1)}, u32[]{:S(2)}, u32[]{:S(2)}) collective-permute-start(f32[48,256]{1,0:T(8,128)S(1)} %get-tuple-element.6), channel_id=1, source_target_pairs={{0,28},{4,24},{8,4},{12,0},{16,12},{20,8},{24,20},{28,16},{1,29},{... | collective-permute-start | bytes 147464 | tf_op jit(solution)/shard_map/ppermute | solution.py:134
  8.8 3.5 %collective-permute-start.2 = (f32[48,256]{1,0:T(8,128)S(1)}, f32[48,256]{1,0:T(8,128)S(1)}, u32[]{:S(2)}, u32[]{:S(2)}) collective-permute-start(f32[48,256]{1,0:T(8,128)S(1)} %get-tuple-element.7), channel_id=1, source_target_pairs={{0,20},{4,16},{8,28},{12,24},{16,4},{20,0},{24,12},{28,8},{1,21},{... | collective-permute-start | bytes 147464 | tf_op jit(solution)/shard_map/ppermute | solution.py:134
  12.3 6.3 %collective-permute-start.4 = (f32[48,256]{1,0:T(8,128)S(1)}, f32[48,256]{1,0:T(8,128)S(1)}, u32[]{:S(2)}, u32[]{:S(2)}) collective-permute-start(f32[48,256]{1,0:T(8,128)S(1)} %fusion.3.own_ref), channel_id=1, source_target_pairs={{0,18},{1,19},{2,16},{3,17},{4,22},{5,23},{6,20},{7,21},{8,26},{9,... | collective-permute-start | bytes 147464 | tf_op jit(solution)/shard_map/ppermute | solution.py:138

commit v4 on v3

--- a/solution.py
+++ b/solution.py
@@ -76,7 +76,7 @@
     operands = [pltpu.with_memory_space_constraint(x, pltpu.HBM) for x in (mask, amplitudes, integrals)]
     return pl.pallas_call(
         functools.partial(ladder_kernel, place),
-        out_shape=jax.ShapeDtypeStruct((2, parts // 2, cols // parts, rows), jnp.float32),
+        out_shape=jax.ShapeDtypeStruct((parts, cols // parts, rows), jnp.float32),
         in_specs=[pl.BlockSpec(memory_space=pltpu.HBM)] * 3,
         out_specs=pl.BlockSpec(memory_space=pltpu.VMEM),
         scratch_shapes=[
@@ -118,24 +118,35 @@
 def shards(amplitudes, integrals, tile_mask, mirror_row):
     n, g = lax.axis_size("virt"), lax.axis_size("pair")
     chips = n // 2
+    rest = chips - 1
 
     def place(b):
         v = lax.axis_index("virt")
         side, chip = lax.rem(v, 2), lax.div(v, 2)
-        s = lax.rem(b // 2 - chip + chips, chips)
-        sender = jnp.where(s == 0, b % 2, 1 - b % 2)
-        return jnp.where(sender == side, 0, 1), s
+        s = (b // 2) ^ chip
+        keeper = jnp.where(s == 0, b % 2, 1 - b % 2)
+        spot = jnp.where(keeper == side, 0, rest) + jnp.where(s == 0, 0, s - 1)
+        return jnp.where(s == 1, 2 * rest + b % 2, spot)
 
-    both = ladder(n, place, tile_mask.T, amplitudes, integrals)
-    mine = both[0] + lax.ppermute(both[1], "virt", [(i, i ^ 1) for i in range(n)])
-    reduced = mine[0]
-    came = []
-    for s in range(1, chips):
-        came.append(lax.ppermute(mine[s], "virt", [(i, ((i + 2 * s) % n) ^ 1) for i in range(n)]))
+    def route(s):
+        return [(i, i ^ (2 * s + 1)) for i in range(n)]
+
+    swap = [(i, i ^ 1) for i in range(n)]
+    blocks = ladder(n, place, tile_mask.T, amplitudes, integrals)
+    arrived = lax.ppermute(blocks[rest:2 * rest], "virt", swap)
+    early = lax.ppermute(blocks[2 * rest:], "virt", route(1))
+    mine = blocks[:rest] + arrived
+    came = [lax.ppermute(mine[s - 1], "virt", route(s)) for s in range(2, chips)]
+    if came:
+        early, came[0] = lax.optimization_barrier((early, came[0]))
+    side = lax.axis_index("virt") % 2
+    keep = lax.dynamic_index_in_dim(early, side, 0, keepdims=False)
+    give = lax.dynamic_index_in_dim(early, 1 - side, 0, keepdims=False)
+    reduced = mine[0] + keep + lax.ppermute(give, "virt", swap)
     for block in came:
         reduced = reduced + block
-    route = [(i * g + q, ((i + chips) % n) * g + (q + g // 2) % g) for i in range(n) for q in range(g)]
-    turned = lax.ppermute(reduced, ("virt", "pair"), route)
+    over = [(i * g + q, (i + chips) % n * g + (q + g // 2) % g) for i in range(n) for q in range(g)]
+    turned = lax.ppermute(reduced, ("virt", "pair"), over)
     return finish(mirror_row.reshape(1, -1), reduced, turned).T
 
 

time: 19.5 us -> 19.2 us (0.985)
  starting transfers between devices: 10 us -> 8.83 us
  waiting for transfers between devices: 5.02 us -> 5.99 us
    ppermute x5 -> x6, starting transfers between devices: 10 us -> 8.83 us  [the longest x1 3.1 us: shards(): turned = lax.ppermute(reduced, ('virt', 'pair'), over)]
    ppermute x5 -> x6, waiting for transfers between devices: 5.02 us -> 5.99 us  [the longest x1 2.9 us: shards(): turned = lax.ppermute(reduced, ('virt', 'pair'), over)]
  transfers between devices with their start and end apart: 5 -> 6, of which waited for: 5 -> 4; matrix products, arithmetic and copies ran while one was open for 0% -> 0% of each run, Pallas kernels for 0% -> 0%
where the time goes in v4:
time: 19.2 us; the launch traced here: 19.1 us
  starting transfers between devices  8.83 us (46%)
  waiting for transfers between devices  5.99 us (31%)
  Pallas kernels  4.17 us (22%)
    pallas_call x1, Pallas kernels, ladder(): pl.pallas_call(functools.partial(ladder_kernel, place), out_shape=jax.Sha...  3.44 us
    ppermute x1, starting transfers between devices, shards(): turned = lax.ppermute(reduced, ('virt', 'pair'), over)  3.1 us
    ppermute x1, waiting for transfers between devices, shards(): turned = lax.ppermute(reduced, ('virt', 'pair'), over)  2.9 us
    ppermute x1, starting transfers between devices, shards(): early = lax.ppermute(blocks[2 * rest:], 'virt', route(1))  2.66 us
    ppermute x2, starting transfers between devices, shards(): lax.ppermute(mine[s - 1], 'virt', route(s))  2.43 us
    ppermute x2, waiting for transfers between devices, shards(): lax.ppermute(mine[s - 1], 'virt', route(s))  2.42 us
    pallas_call x1, Pallas kernels, finish(): pl.pallas_call(finish_kernel, out_shape=jax.ShapeDtypeStruct(own.shape, o...  0.73 us
    ppermute x1, waiting for transfers between devices, shards(): early = lax.ppermute(blocks[2 * rest:], 'virt', route(1))  0.67 us
  transfers between devices with their start and end apart: 6, of which 4 were waited for; matrix products, arithmetic and copies ran while one was open for 0% of the time, Pallas kernels for 0%

profile of v4, /device:TPU:0, one launch (start us, length us, event | category | flops | bytes accessed | tf_op | source)
XLA Modules:
  0.0 19.1 jit_solution(17503729720967604664)
XLA Ops:
  0.0 0.0 copy-start
  0.0 3.4 %ladder.1 = f32[8,48,256]{2,1,0:T(8,128)S(1)} custom-call(s32[4,20]{1,0:T(4,128)} %bitcast.18, f32[256,1920]{1,0:T(8,128)} %amp_hbm.1, f32[1920,384]{1,0:T(8,128)} %int_hbm.1), custom_call_target="tpu_custom_call" | custom-call | tf_op jit(solution)/shard_map/ladder/pallas_call | solution.py:77
  3.5 0.5 %collective-permute-start = (f32[3,48,256]{2,1,0:T(8,128)S(1)}, f32[3,48,256]{2,1,0:T(8,128)S(1)}, u32[]{:S(2)}, u32[]{:S(2)}) collective-permute-start(f32[3,48,256]{2,1,0:T(8,128)S(1)} %slice.25), channel_id=1, source_target_pairs={{0,4},{4,0},{8,12},{12,8},{16,20},{20,16},{24,28},{28,24},{1,5},{5... | collective-permute-start | bytes 442376 | tf_op jit(solution)/shard_map/ppermute | solution.py:136
  4.0 2.7 %collective-permute-start.1 = (f32[2,48,256]{2,1,0:T(8,128)S(1)}, f32[2,48,256]{2,1,0:T(8,128)S(1)}, u32[]{:S(2)}, u32[]{:S(2)}) collective-permute-start(f32[2,48,256]{2,1,0:T(8,128)S(1)} %slice.27), channel_id=1, source_target_pairs={{0,12},{4,8},{8,4},{12,0},{16,28},{20,24},{24,20},{28,16},{1,13},{... | collective-permute-start | bytes 294920 | tf_op jit(solution)/shard_map/ppermute | solution.py:137
  6.7 0.0 collective-permute-done
  6.7 1.2 %collective-permute-start.2 = (f32[48,256]{1,0:T(8,128)S(1)}, f32[48,256]{1,0:T(8,128)S(1)}, u32[]{:S(2)}, u32[]{:S(2)}) collective-permute-start(f32[48,256]{1,0:T(8,128)S(1)} %get-tuple-element.9), channel_id=1, source_target_pairs={{0,20},{4,16},{8,28},{12,24},{16,4},{20,0},{24,12},{28,8},{1,21},{... | collective-permute-start | bytes 147464 | tf_op jit(solution)/shard_map/ppermute | solution.py:139
  7.9 1.2 %collective-permute-start.4 = (f32[48,256]{1,0:T(8,128)S(1)}, f32[48,256]{1,0:T(8,128)S(1)}, u32[]{:S(2)}, u32[]{:S(2)}) collective-permute-start(f32[48,256]{1,0:T(8,128)S(1)} %get-tuple-element.10), channel_id=1, source_target_pairs={{0,28},{4,24},{8,20},{12,16},{16,12},{20,8},{24,4},{28,0},{1,29},{... | collective-permute-start | bytes 147464 | tf_op jit(solution)/shard_map/ppermute | solution.py:139
  9.1 0.7 %collective-permute-done.1 = f32[2,48,256]{2,1,0:T(8,128)S(1)} collective-permute-done((f32[2,48,256]{2,1,0:T(8,128)S(1)}, f32[2,48,256]{2,1,0:T(8,128)S(1)}, u32[]{:S(2)}, u32[]{:S(2)}) %collective-permute-start.1) | collective-permute-done | bytes 98336 | tf_op jit(solution)/shard_map/ppermute | solution.py:137
  9.8 0.8 %collective-permute-done.2 = f32[48,256]{1,0:T(8,128)S(1)} collective-permute-done((f32[48,256]{1,0:T(8,128)S(1)}, f32[48,256]{1,0:T(8,128)S(1)}, u32[]{:S(2)}, u32[]{:S(2)}) %collective-permute-start.2) | collective-permute-done | bytes 49184 | tf_op jit(solution)/shard_map/ppermute | solution.py:139
  10.6 0.1 collective-permute-start.3
  10.7 1.6 %collective-permute-done.4 = f32[48,256]{1,0:T(8,128)S(1)} collective-permute-done((f32[48,256]{1,0:T(8,128)S(1)}, f32[48,256]{1,0:T(8,128)S(1)}, u32[]{:S(2)}, u32[]{:S(2)}) %collective-permute-start.4) | collective-permute-done | bytes 49184 | tf_op jit(solution)/shard_map/ppermute | solution.py:139
  12.3 0.0 collective-permute-done.3
  12.4 3.1 %collective-permute-start.5 = (f32[48,256]{1,0:T(8,128)S(1)}, f32[48,256]{1,0:T(8,128)S(1)}, u32[]{:S(2)}, u32[]{:S(2)}) collective-permute-start(f32[48,256]{1,0:T(8,128)S(1)} %fusion.3.own_ref), channel_id=1, source_target_pairs={{0,18},{1,19},{2,16},{3,17},{4,22},{5,23},{6,20},{7,21},{8,26},{9,... | collective-permute-start | bytes 147464 | tf_op jit(solution)/shard_map/ppermute | solution.py:149
  15.5 2.9 %collective-permute-done.5.other_ref = f32[48,256]{1,0:T(8,128)S(1)} collective-permute-done((f32[48,256]{1,0:T(8,128)S(1)}, f32[48,256]{1,0:T(8,128)S(1)}, u32[]{:S(2)}, u32[]{:S(2)}) %collective-permute-start.5) | collective-permute-done | bytes 49184 | tf_op jit(solution)/shard_map/ppermute | solution.py:149
  18.4 0.0 copy-done
  18.4 0.7 %finish.1 = f32[48,256]{1,0:T(8,128)} custom-call(s32[1,256]{1,0:T(1,128)S(1)} %bitcast.17, f32[48,256]{1,0:T(8,128)S(1)} %fusion.3.own_ref, f32[48,256]{1,0:T(8,128)S(1)} %collective-permute-done.5.other_ref), custom_call_target="tpu_custom_call" | custom-call | tf_op jit(solution)/shard_map/finish/pallas_call | solution.py:108
  (6 shorter events, 0.1 us)
Async XLA Ops:
  0.0 18.4 %copy-start = (s32[256]{0:T(256)S(1)}, s32[256]{0:T(256)}, u32[]{:S(2)}) copy-start(s32[256]{0:T(256)} %param.7) | copy-start | bytes 3076
  3.5 3.2 %collective-permute-start = (f32[3,48,256]{2,1,0:T(8,128)S(1)}, f32[3,48,256]{2,1,0:T(8,128)S(1)}, u32[]{:S(2)}, u32[]{:S(2)}) collective-permute-start(f32[3,48,256]{2,1,0:T(8,128)S(1)} %slice.25), channel_id=1, source_target_pairs={{0,4},{4,0},{8,12},{12,8},{16,20},{20,16},{24,28},{28,24},{1,5},{5... | collective-permute-start | bytes 442376 | tf_op jit(solution)/shard_map/ppermute | solution.py:136
  4.0 5.8 %collective-permute-start.1 = (f32[2,48,256]{2,1,0:T(8,128)S(1)}, f32[2,48,256]{2,1,0:T(8,128)S(1)}, u32[]{:S(2)}, u32[]{:S(2)}) collective-permute-start(f32[2,48,256]{2,1,0:T(8,128)S(1)} %slice.27), channel_id=1, source_target_pairs={{0,12},{4,8},{8,4},{12,0},{16,28},{20,24},{24,20},{28,16},{1,13},{... | collective-permute-start | bytes 294920 | tf_op jit(solution)/shard_map/ppermute | solution.py:137
  6.7 3.9 %collective-permute-start.2 = (f32[48,256]{1,0:T(8,128)S(1)}, f32[48,256]{1,0:T(8,128)S(1)}, u32[]{:S(2)}, u32[]{:S(2)}) collective-permute-start(f32[48,256]{1,0:T(8,128)S(1)} %get-tuple-element.9), channel_id=1, source_target_pairs={{0,20},{4,16},{8,28},{12,24},{16,4},{20,0},{24,12},{28,8},{1,21},{... | collective-permute-start | bytes 147464 | tf_op jit(solution)/shard_map/ppermute | solution.py:139
  7.9 4.4 %collective-permute-start.4 = (f32[48,256]{1,0:T(8,128)S(1)}, f32[48,256]{1,0:T(8,128)S(1)}, u32[]{:S(2)}, u32[]{:S(2)}) collective-permute-start(f32[48,256]{1,0:T(8,128)S(1)} %get-tuple-element.10), channel_id=1, source_target_pairs={{0,28},{4,24},{8,20},{12,16},{16,12},{20,8},{24,4},{28,0},{1,29},{... | collective-permute-start | bytes 147464 | tf_op jit(solution)/shard_map/ppermute | solution.py:139
  10.6 1.7 %collective-permute-start.3 = (f32[48,256]{1,0:T(8,128)S(1)}, f32[48,256]{1,0:T(8,128)S(1)}, u32[]{:S(2)}, u32[]{:S(2)}) collective-permute-start(f32[48,256]{1,0:T(8,128)S(1)} %dynamic-slice_bitcast_fusion), channel_id=1, source_target_pairs={{0,4},{4,0},{8,12},{12,8},{16,20},{20,16},{24,28},{28,24},{1,5},{5... | collective-permute-start | bytes 147464 | tf_op jit(solution)/shard_map/ppermute | solution.py:145
  12.4 6.0 %collective-permute-start.5 = (f32[48,256]{1,0:T(8,128)S(1)}, f32[48,256]{1,0:T(8,128)S(1)}, u32[]{:S(2)}, u32[]{:S(2)}) collective-permute-start(f32[48,256]{1,0:T(8,128)S(1)} %fusion.3.own_ref), channel_id=1, source_target_pairs={{0,18},{1,19},{2,16},{3,17},{4,22},{5,23},{6,20},{7,21},{8,26},{9,... | collective-permute-start | bytes 147464 | tf_op jit(solution)/shard_map/ppermute | solution.py:149

commit v5 on v4

--- a/solution.py
+++ b/solution.py
@@ -91,7 +91,7 @@
     )(*operands)
 
 
-def finish_kernel(mirror_ref, own_ref, other_ref, out_ref):
+def finish_kernel(mirror_ref, other_ref, own_ref, out_ref):
     rows = own_ref.shape[1]
     lanes = 128
     for j in range(0, rows, lanes):
@@ -104,7 +104,7 @@
         out_ref[:, j:j + lanes] = picked
 
 
-def finish(mirror, own, other):
+def finish(mirror, other, own):
     return pl.pallas_call(
         finish_kernel,
         out_shape=jax.ShapeDtypeStruct(own.shape, own.dtype),
@@ -112,42 +112,50 @@
         out_specs=pl.BlockSpec(memory_space=pltpu.VMEM),
         compiler_params=pltpu.CompilerParams(vmem_limit_bytes=4 * MIB),
         name="finish",
-    )(mirror, own, other)
+    )(mirror, other, own)
 
 
 def shards(amplitudes, integrals, tile_mask, mirror_row):
     n, g = lax.axis_size("virt"), lax.axis_size("pair")
     chips = n // 2
     rest = chips - 1
+    ring = [i ^ (i >> 1) for i in range(chips)]
+    if sorted(ring) != list(range(chips)):
+        ring = list(range(chips))
+    distances = [d for near in range(1, chips // 2 + 1) for d in (near, chips - near)][:rest]
 
     def place(b):
         v = lax.axis_index("virt")
         side, chip = lax.rem(v, 2), lax.div(v, 2)
-        s = (b // 2) ^ chip
-        keeper = jnp.where(s == 0, b % 2, 1 - b % 2)
-        spot = jnp.where(keeper == side, 0, rest) + jnp.where(s == 0, 0, s - 1)
-        return jnp.where(s == 1, 2 * rest + b % 2, spot)
+        here = sum(jnp.where(chip == c, ring.index(c), 0) for c in range(chips))
+        ahead = lax.rem(ring.index(b // 2) - here + chips, chips)
+        step = jnp.where(2 * ahead > chips, 2 * (chips - ahead), jnp.maximum(2 * ahead - 1, 0))
+        keeper = jnp.where(step == 0, 1 - b % 2, b % 2)
+        spot = jnp.where(keeper == side, 0, rest) + jnp.maximum(step - 1, 0)
+        return jnp.where(step == 1, 2 * rest + b % 2, spot)
 
-    def route(s):
-        return [(i, i ^ (2 * s + 1)) for i in range(n)]
+    def route(step):
+        ahead = distances[step - 1]
+        return [(2 * ring[p] + k, 2 * ring[(p + ahead) % chips] + 1 - k) for p in range(chips) for k in range(2)]
 
     swap = [(i, i ^ 1) for i in range(n)]
     blocks = ladder(n, place, tile_mask.T, amplitudes, integrals)
     arrived = lax.ppermute(blocks[rest:2 * rest], "virt", swap)
     early = lax.ppermute(blocks[2 * rest:], "virt", route(1))
     mine = blocks[:rest] + arrived
-    came = [lax.ppermute(mine[s - 1], "virt", route(s)) for s in range(2, chips)]
+    came = [lax.ppermute(mine[step - 1], "virt", route(step)) for step in range(2, chips)]
     if came:
         early, came[0] = lax.optimization_barrier((early, came[0]))
     side = lax.axis_index("virt") % 2
-    keep = lax.dynamic_index_in_dim(early, side, 0, keepdims=False)
-    give = lax.dynamic_index_in_dim(early, 1 - side, 0, keepdims=False)
+    keep = lax.dynamic_index_in_dim(early, 1 - side, 0, keepdims=False)
+    give = lax.dynamic_index_in_dim(early, side, 0, keepdims=False)
     reduced = mine[0] + keep + lax.ppermute(give, "virt", swap)
     for block in came:
         reduced = reduced + block
-    over = [(i * g + q, (i + chips) % n * g + (q + g // 2) % g) for i in range(n) for q in range(g)]
+    over = [(i * g + q, ((i + chips) % n ^ 1) * g + (q + g // 2) % g) for i in range(n) for q in range(g)]
     turned = lax.ppermute(reduced, ("virt", "pair"), over)
-    return finish(mirror_row.reshape(1, -1), reduced, turned).T
+    own = lax.ppermute(reduced, "virt", swap)
+    return finish(mirror_row.reshape(1, -1), turned, own).T
 
 
 def solution(mesh):

time: 19.2 us -> 18.7 us (0.974)
  the two profiles are of different devices: /device:TPU:0 before, /device:TPU:27 now
where the time goes in v5:
time: 18.7 us; the launch traced here: 18.6 us
  waiting for transfers between devices  8.08 us (43%)
  starting transfers between devices  6.21 us (33%)
  Pallas kernels  4.17 us (22%)
    ppermute x1, waiting for transfers between devices, shards(): turned = lax.ppermute(reduced, ('virt', 'pair'), over)  5.47 us
    pallas_call x1, Pallas kernels, ladder(): pl.pallas_call(functools.partial(ladder_kernel, place), out_shape=jax.Sha...  3.44 us
    ppermute x2, starting transfers between devices, shards(): lax.ppermute(mine[step - 1], 'virt', route(step))  2.57 us
    ppermute x2, waiting for transfers between devices, shards(): lax.ppermute(mine[step - 1], 'virt', route(step))  1.64 us
    ppermute x1, starting transfers between devices, shards(): early = lax.ppermute(blocks[2 * rest:], 'virt', route(1))  1.2 us
    ppermute x1, waiting for transfers between devices, shards(): early = lax.ppermute(blocks[2 * rest:], 'virt', route(1))  0.97 us
    ppermute x1, starting transfers between devices, shards(): turned = lax.ppermute(reduced, ('virt', 'pair'), over)  0.96 us
    ppermute x1, starting transfers between devices, shards(): arrived = lax.ppermute(blocks[rest:2 * rest], 'virt', swap)  0.74 us
  transfers between devices with their start and end apart: 7, of which 4 were waited for; matrix products, arithmetic and copies ran while one was open for 0% of the time, Pallas kernels for 0%

profile of v5, /device:TPU:27, one launch (start us, length us, event | category | flops | bytes accessed | tf_op | source)
XLA Modules:
  0.0 18.6 jit_solution(850633660361412083)
XLA Ops:
  0.0 0.0 copy-start
  0.0 3.4 %ladder.1 = f32[8,48,256]{2,1,0:T(8,128)S(1)} custom-call(s32[4,20]{1,0:T(4,128)} %bitcast.18, f32[256,1920]{1,0:T(8,128)} %amp_hbm.1, f32[1920,384]{1,0:T(8,128)} %int_hbm.1), custom_call_target="tpu_custom_call" | custom-call | tf_op jit(solution)/shard_map/ladder/pallas_call | solution.py:77
  3.5 0.7 %collective-permute-start = (f32[3,48,256]{2,1,0:T(8,128)S(1)}, f32[3,48,256]{2,1,0:T(8,128)S(1)}, u32[]{:S(2)}, u32[]{:S(2)}) collective-permute-start(f32[3,48,256]{2,1,0:T(8,128)S(1)} %slice.25), channel_id=1, source_target_pairs={{0,4},{4,0},{8,12},{12,8},{16,20},{20,16},{24,28},{28,24},{1,5},{5... | collective-permute-start | bytes 442376 | tf_op jit(solution)/shard_map/ppermute | solution.py:143
  4.2 1.2 %collective-permute-start.1 = (f32[2,48,256]{2,1,0:T(8,128)S(1)}, f32[2,48,256]{2,1,0:T(8,128)S(1)}, u32[]{:S(2)}, u32[]{:S(2)}) collective-permute-start(f32[2,48,256]{2,1,0:T(8,128)S(1)} %slice.27), channel_id=1, source_target_pairs={{0,12},{4,8},{8,28},{12,24},{24,20},{28,16},{16,4},{20,0},{1,13},{... | collective-permute-start | bytes 294920 | tf_op jit(solution)/shard_map/ppermute | solution.py:144
  5.4 0.0 collective-permute-done
  5.5 0.6 %collective-permute-start.2 = (f32[48,256]{1,0:T(8,128)S(1)}, f32[48,256]{1,0:T(8,128)S(1)}, u32[]{:S(2)}, u32[]{:S(2)}) collective-permute-start(f32[48,256]{1,0:T(8,128)S(1)} %get-tuple-element.9), channel_id=1, source_target_pairs={{0,20},{4,16},{8,4},{12,0},{24,12},{28,8},{16,28},{20,24},{1,21},{... | collective-permute-start | bytes 147464 | tf_op jit(solution)/shard_map/ppermute | solution.py:146
  6.1 1.9 %collective-permute-start.4 = (f32[48,256]{1,0:T(8,128)S(1)}, f32[48,256]{1,0:T(8,128)S(1)}, u32[]{:S(2)}, u32[]{:S(2)}) collective-permute-start(f32[48,256]{1,0:T(8,128)S(1)} %get-tuple-element.10), channel_id=1, source_target_pairs={{0,28},{4,24},{8,20},{12,16},{24,4},{28,0},{16,12},{20,8},{1,29},{... | collective-permute-start | bytes 147464 | tf_op jit(solution)/shard_map/ppermute | solution.py:146
  8.0 1.0 %collective-permute-done.1 = f32[2,48,256]{2,1,0:T(8,128)S(1)} collective-permute-done((f32[2,48,256]{2,1,0:T(8,128)S(1)}, f32[2,48,256]{2,1,0:T(8,128)S(1)}, u32[]{:S(2)}, u32[]{:S(2)}) %collective-permute-start.1) | collective-permute-done | bytes 98336 | tf_op jit(solution)/shard_map/ppermute | solution.py:144
  9.0 0.4 %collective-permute-done.2 = f32[48,256]{1,0:T(8,128)S(1)} collective-permute-done((f32[48,256]{1,0:T(8,128)S(1)}, f32[48,256]{1,0:T(8,128)S(1)}, u32[]{:S(2)}, u32[]{:S(2)}) %collective-permute-start.2) | collective-permute-done | bytes 49184 | tf_op jit(solution)/shard_map/ppermute | solution.py:146
  9.4 0.4 %collective-permute-start.3 = (f32[48,256]{1,0:T(8,128)S(1)}, f32[48,256]{1,0:T(8,128)S(1)}, u32[]{:S(2)}, u32[]{:S(2)}) collective-permute-start(f32[48,256]{1,0:T(8,128)S(1)} %dynamic-slice_bitcast_fusion), channel_id=1, source_target_pairs={{0,4},{4,0},{8,12},{12,8},{16,20},{20,16},{24,28},{28,24},{1,5},{5... | collective-permute-start | bytes 147464 | tf_op jit(solution)/shard_map/ppermute | solution.py:152
  9.8 1.2 %collective-permute-done.4 = f32[48,256]{1,0:T(8,128)S(1)} collective-permute-done((f32[48,256]{1,0:T(8,128)S(1)}, f32[48,256]{1,0:T(8,128)S(1)}, u32[]{:S(2)}, u32[]{:S(2)}) %collective-permute-start.4) | collective-permute-done | bytes 49184 | tf_op jit(solution)/shard_map/ppermute | solution.py:146
  11.0 0.0 collective-permute-done.3
  11.1 1.0 %collective-permute-start.5 = (f32[48,256]{1,0:T(8,128)S(1)}, f32[48,256]{1,0:T(8,128)S(1)}, u32[]{:S(2)}, u32[]{:S(2)}) collective-permute-start(f32[48,256]{1,0:T(8,128)S(1)} %fusion.3), channel_id=1, source_target_pairs={{0,22},{1,23},{2,20},{3,21},{4,18},{5,19},{6,16},{7,17},{8,30},{9,... | collective-permute-start | bytes 147464 | tf_op jit(solution)/shard_map/ppermute | solution.py:156
  12.0 0.3 %collective-permute-start.6 = (f32[48,256]{1,0:T(8,128)S(1)}, f32[48,256]{1,0:T(8,128)S(1)}, u32[]{:S(2)}, u32[]{:S(2)}) collective-permute-start(f32[48,256]{1,0:T(8,128)S(1)} %fusion.3), channel_id=1, source_target_pairs={{0,4},{4,0},{8,12},{12,8},{16,20},{20,16},{24,28},{28,24},{1,5},{5... | collective-permute-start | bytes 147464 | tf_op jit(solution)/shard_map/ppermute | solution.py:157
  12.4 5.5 %collective-permute-done.5.other_ref = f32[48,256]{1,0:T(8,128)S(1)} collective-permute-done((f32[48,256]{1,0:T(8,128)S(1)}, f32[48,256]{1,0:T(8,128)S(1)}, u32[]{:S(2)}, u32[]{:S(2)}) %collective-permute-start.5) | collective-permute-done | bytes 49184 | tf_op jit(solution)/shard_map/ppermute | solution.py:156
  17.8 0.0 collective-permute-done.6.own_ref
  17.8 0.0 copy-done
  17.9 0.7 %finish.1 = f32[48,256]{1,0:T(8,128)} custom-call(s32[1,256]{1,0:T(1,128)S(1)} %bitcast.17, f32[48,256]{1,0:T(8,128)S(1)} %collective-permute-done.5.other_ref, f32[48,256]{1,0:T(8,128)S(1)} %collective-permute-done.6.own_ref), custom_call_target="tpu_custom_call" | custom-call | tf_op jit(solution)/shard_map/finish/pallas_call | solution.py:108
  (6 shorter events, 0.1 us)
Async XLA Ops:
  0.0 17.9 %copy-start = (s32[256]{0:T(256)S(1)}, s32[256]{0:T(256)}, u32[]{:S(2)}) copy-start(s32[256]{0:T(256)} %param.7) | copy-start | bytes 3076
  3.5 1.9 %collective-permute-start = (f32[3,48,256]{2,1,0:T(8,128)S(1)}, f32[3,48,256]{2,1,0:T(8,128)S(1)}, u32[]{:S(2)}, u32[]{:S(2)}) collective-permute-start(f32[3,48,256]{2,1,0:T(8,128)S(1)} %slice.25), channel_id=1, source_target_pairs={{0,4},{4,0},{8,12},{12,8},{16,20},{20,16},{24,28},{28,24},{1,5},{5... | collective-permute-start | bytes 442376 | tf_op jit(solution)/shard_map/ppermute | solution.py:143
  4.2 4.8 %collective-permute-start.1 = (f32[2,48,256]{2,1,0:T(8,128)S(1)}, f32[2,48,256]{2,1,0:T(8,128)S(1)}, u32[]{:S(2)}, u32[]{:S(2)}) collective-permute-start(f32[2,48,256]{2,1,0:T(8,128)S(1)} %slice.27), channel_id=1, source_target_pairs={{0,12},{4,8},{8,28},{12,24},{24,20},{28,16},{16,4},{20,0},{1,13},{... | collective-permute-start | bytes 294920 | tf_op jit(solution)/shard_map/ppermute | solution.py:144
  5.5 4.0 %collective-permute-start.2 = (f32[48,256]{1,0:T(8,128)S(1)}, f32[48,256]{1,0:T(8,128)S(1)}, u32[]{:S(2)}, u32[]{:S(2)}) collective-permute-start(f32[48,256]{1,0:T(8,128)S(1)} %get-tuple-element.9), channel_id=1, source_target_pairs={{0,20},{4,16},{8,4},{12,0},{24,12},{28,8},{16,28},{20,24},{1,21},{... | collective-permute-start | bytes 147464 | tf_op jit(solution)/shard_map/ppermute | solution.py:146
  6.1 4.9 %collective-permute-start.4 = (f32[48,256]{1,0:T(8,128)S(1)}, f32[48,256]{1,0:T(8,128)S(1)}, u32[]{:S(2)}, u32[]{:S(2)}) collective-permute-start(f32[48,256]{1,0:T(8,128)S(1)} %get-tuple-element.10), channel_id=1, source_target_pairs={{0,28},{4,24},{8,20},{12,16},{24,4},{28,0},{16,12},{20,8},{1,29},{... | collective-permute-start | bytes 147464 | tf_op jit(solution)/shard_map/ppermute | solution.py:146
  9.4 1.6 %collective-permute-start.3 = (f32[48,256]{1,0:T(8,128)S(1)}, f32[48,256]{1,0:T(8,128)S(1)}, u32[]{:S(2)}, u32[]{:S(2)}) collective-permute-start(f32[48,256]{1,0:T(8,128)S(1)} %dynamic-slice_bitcast_fusion), channel_id=1, source_target_pairs={{0,4},{4,0},{8,12},{12,8},{16,20},{20,16},{24,28},{28,24},{1,5},{5... | collective-permute-start | bytes 147464 | tf_op jit(solution)/shard_map/ppermute | solution.py:152
  11.1 6.8 %collective-permute-start.5 = (f32[48,256]{1,0:T(8,128)S(1)}, f32[48,256]{1,0:T(8,128)S(1)}, u32[]{:S(2)}, u32[]{:S(2)}) collective-permute-start(f32[48,256]{1,0:T(8,128)S(1)} %fusion.3), channel_id=1, source_target_pairs={{0,22},{1,23},{2,20},{3,21},{4,18},{5,19},{6,16},{7,17},{8,30},{9,... | collective-permute-start | bytes 147464 | tf_op jit(solution)/shard_map/ppermute | solution.py:156
  12.0 5.8 %collective-permute-start.6 = (f32[48,256]{1,0:T(8,128)S(1)}, f32[48,256]{1,0:T(8,128)S(1)}, u32[]{:S(2)}, u32[]{:S(2)}) collective-permute-start(f32[48,256]{1,0:T(8,128)S(1)} %fusion.3), channel_id=1, source_target_pairs={{0,4},{4,0},{8,12},{12,8},{16,20},{20,16},{24,28},{28,24},{1,5},{5... | collective-permute-start | bytes 147464 | tf_op jit(solution)/shard_map/ppermute | solution.py:157

commit v6 on v5

--- a/solution.py
+++ b/solution.py
@@ -128,7 +128,9 @@
         v = lax.axis_index("virt")
         side, chip = lax.rem(v, 2), lax.div(v, 2)
         here = sum(jnp.where(chip == c, ring.index(c), 0) for c in range(chips))
-        ahead = lax.rem(ring.index(b // 2) - here + chips, chips)
+        opposite = ring.index((b // 2 + chips // 2) % chips)
+        there = jnp.where(lax.axis_index("pair") > 0, opposite, ring.index(b // 2))
+        ahead = lax.rem(there - here + chips, chips)
         step = jnp.where(2 * ahead > chips, 2 * (chips - ahead), jnp.maximum(2 * ahead - 1, 0))
         keeper = jnp.where(step == 0, 1 - b % 2, b % 2)
         spot = jnp.where(keeper == side, 0, rest) + jnp.maximum(step - 1, 0)
@@ -152,9 +154,13 @@
     reduced = mine[0] + keep + lax.ppermute(give, "virt", swap)
     for block in came:
         reduced = reduced + block
-    over = [(i * g + q, ((i + chips) % n ^ 1) * g + (q + g // 2) % g) for i in range(n) for q in range(g)]
-    turned = lax.ppermute(reduced, ("virt", "pair"), over)
-    own = lax.ppermute(reduced, "virt", swap)
+    def owner(i, q):
+        return (i + (chips if q > 0 else 0)) % n ^ 1
+
+    across = [(i * g + q, (owner(i, q) + chips) % n * g + (q + g // 2) % g) for i in range(n) for q in range(g)]
+    home = [(i * g + q, owner(i, q) * g + q) for i in range(n) for q in range(g)]
+    turned = lax.ppermute(reduced, ("virt", "pair"), across)
+    own = lax.ppermute(reduced, ("virt", "pair"), home)
     return finish(mirror_row.reshape(1, -1), turned, own).T
 
 

time: 18.7 us -> 18.3 us (0.979)
  the two profiles are of different devices: /device:TPU:27 before, /device:TPU:0 now
where the time goes in v6:
time: 18.3 us; the launch traced here: 18.2 us
  starting transfers between devices  9.73 us (53%)
  Pallas kernels  4.17 us (23%)
  waiting for transfers between devices  4.17 us (23%)
    ppermute x1, starting transfers between devices, shards(): turned = lax.ppermute(reduced, ('virt', 'pair'), across)  3.52 us
    pallas_call x1, Pallas kernels, ladder(): pl.pallas_call(functools.partial(ladder_kernel, place), out_shape=jax.Sha...  3.44 us
    ppermute x2, starting transfers between devices, shards(): lax.ppermute(mine[step - 1], 'virt', route(step))  2.76 us
    ppermute x1, starting transfers between devices, shards(): early = lax.ppermute(blocks[2 * rest:], 'virt', route(1))  2.65 us
    ppermute x2, waiting for transfers between devices, shards(): lax.ppermute(mine[step - 1], 'virt', route(step))  2.21 us
    ppermute x1, waiting for transfers between devices, shards(): turned = lax.ppermute(reduced, ('virt', 'pair'), across)  1.59 us
    pallas_call x1, Pallas kernels, finish(): pl.pallas_call(finish_kernel, out_shape=jax.ShapeDtypeStruct(own.shape, o...  0.73 us
    ppermute x1, starting transfers between devices, shards(): arrived = lax.ppermute(blocks[rest:2 * rest], 'virt', swap)  0.52 us
  transfers between devices with their start and end apart: 7, of which 4 were waited for; matrix products, arithmetic and copies ran while one was open for 0% of the time, Pallas kernels for 0%

profile of v6, /device:TPU:0, one launch (start us, length us, event | category | flops | bytes accessed | tf_op | source)
XLA Modules:
  0.0 18.2 jit_solution(14979713121109921354)
XLA Ops:
  0.0 0.0 copy-start
  0.0 3.4 %ladder.1 = f32[8,48,256]{2,1,0:T(8,128)S(1)} custom-call(s32[4,20]{1,0:T(4,128)} %bitcast.18, f32[256,1920]{1,0:T(8,128)} %amp_hbm.1, f32[1920,384]{1,0:T(8,128)} %int_hbm.1), custom_call_target="tpu_custom_call" | custom-call | tf_op jit(solution)/shard_map/ladder/pallas_call | solution.py:77
  3.5 0.5 %collective-permute-start = (f32[3,48,256]{2,1,0:T(8,128)S(1)}, f32[3,48,256]{2,1,0:T(8,128)S(1)}, u32[]{:S(2)}, u32[]{:S(2)}) collective-permute-start(f32[3,48,256]{2,1,0:T(8,128)S(1)} %slice.25), channel_id=1, source_target_pairs={{0,4},{4,0},{8,12},{12,8},{16,20},{20,16},{24,28},{28,24},{1,5},{5... | collective-permute-start | bytes 442376 | tf_op jit(solution)/shard_map/ppermute | solution.py:145
  4.0 2.6 %collective-permute-start.1 = (f32[2,48,256]{2,1,0:T(8,128)S(1)}, f32[2,48,256]{2,1,0:T(8,128)S(1)}, u32[]{:S(2)}, u32[]{:S(2)}) collective-permute-start(f32[2,48,256]{2,1,0:T(8,128)S(1)} %slice.27), channel_id=1, source_target_pairs={{0,12},{4,8},{8,28},{12,24},{24,20},{28,16},{16,4},{20,0},{1,13},{... | collective-permute-start | bytes 294920 | tf_op jit(solution)/shard_map/ppermute | solution.py:146
  6.6 0.0 collective-permute-done
  6.7 1.0 %collective-permute-start.2 = (f32[48,256]{1,0:T(8,128)S(1)}, f32[48,256]{1,0:T(8,128)S(1)}, u32[]{:S(2)}, u32[]{:S(2)}) collective-permute-start(f32[48,256]{1,0:T(8,128)S(1)} %get-tuple-element.9), channel_id=1, source_target_pairs={{0,20},{4,16},{8,4},{12,0},{24,12},{28,8},{16,28},{20,24},{1,21},{... | collective-permute-start | bytes 147464 | tf_op jit(solution)/shard_map/ppermute | solution.py:148
  7.7 1.7 %collective-permute-start.4 = (f32[48,256]{1,0:T(8,128)S(1)}, f32[48,256]{1,0:T(8,128)S(1)}, u32[]{:S(2)}, u32[]{:S(2)}) collective-permute-start(f32[48,256]{1,0:T(8,128)S(1)} %get-tuple-element.10), channel_id=1, source_target_pairs={{0,28},{4,24},{8,20},{12,16},{24,4},{28,0},{16,12},{20,8},{1,29},{... | collective-permute-start | bytes 147464 | tf_op jit(solution)/shard_map/ppermute | solution.py:148
  9.5 0.4 %collective-permute-done.1 = f32[2,48,256]{2,1,0:T(8,128)S(1)} collective-permute-done((f32[2,48,256]{2,1,0:T(8,128)S(1)}, f32[2,48,256]{2,1,0:T(8,128)S(1)}, u32[]{:S(2)}, u32[]{:S(2)}) %collective-permute-start.1) | collective-permute-done | bytes 98336 | tf_op jit(solution)/shard_map/ppermute | solution.py:146
  9.8 0.8 %collective-permute-done.2 = f32[48,256]{1,0:T(8,128)S(1)} collective-permute-done((f32[48,256]{1,0:T(8,128)S(1)}, f32[48,256]{1,0:T(8,128)S(1)}, u32[]{:S(2)}, u32[]{:S(2)}) %collective-permute-start.2) | collective-permute-done | bytes 49184 | tf_op jit(solution)/shard_map/ppermute | solution.py:148
  10.6 0.1 collective-permute-start.3
  10.7 1.4 %collective-permute-done.4 = f32[48,256]{1,0:T(8,128)S(1)} collective-permute-done((f32[48,256]{1,0:T(8,128)S(1)}, f32[48,256]{1,0:T(8,128)S(1)}, u32[]{:S(2)}, u32[]{:S(2)}) %collective-permute-start.4) | collective-permute-done | bytes 49184 | tf_op jit(solution)/shard_map/ppermute | solution.py:148
  12.1 0.0 collective-permute-done.3
  12.2 3.5 %collective-permute-start.5 = (f32[48,256]{1,0:T(8,128)S(1)}, f32[48,256]{1,0:T(8,128)S(1)}, u32[]{:S(2)}, u32[]{:S(2)}) collective-permute-start(f32[48,256]{1,0:T(8,128)S(1)} %fusion.3), channel_id=1, source_target_pairs={{0,22},{1,7},{2,4},{3,5},{4,18},{5,3},{6,0},{7,1},{8,30},{9,15},{1... | collective-permute-start | bytes 147464 | tf_op jit(solution)/shard_map/ppermute | solution.py:162
  15.7 0.2 collective-permute-start.6
  15.9 1.6 %collective-permute-done.5.other_ref = f32[48,256]{1,0:T(8,128)S(1)} collective-permute-done((f32[48,256]{1,0:T(8,128)S(1)}, f32[48,256]{1,0:T(8,128)S(1)}, u32[]{:S(2)}, u32[]{:S(2)}) %collective-permute-start.5) | collective-permute-done | bytes 49184 | tf_op jit(solution)/shard_map/ppermute | solution.py:162
  17.4 0.0 collective-permute-done.6.own_ref
  17.4 0.0 copy-done
  17.5 0.7 %finish.1 = f32[48,256]{1,0:T(8,128)} custom-call(s32[1,256]{1,0:T(1,128)S(1)} %bitcast.17, f32[48,256]{1,0:T(8,128)S(1)} %collective-permute-done.5.other_ref, f32[48,256]{1,0:T(8,128)S(1)} %collective-permute-done.6.own_ref), custom_call_target="tpu_custom_call" | custom-call | tf_op jit(solution)/shard_map/finish/pallas_call | solution.py:108
  (6 shorter events, 0.1 us)
Async XLA Ops:
  0.0 17.4 %copy-start = (s32[256]{0:T(256)S(1)}, s32[256]{0:T(256)}, u32[]{:S(2)}) copy-start(s32[256]{0:T(256)} %param.7) | copy-start | bytes 3076
  3.5 3.2 %collective-permute-start = (f32[3,48,256]{2,1,0:T(8,128)S(1)}, f32[3,48,256]{2,1,0:T(8,128)S(1)}, u32[]{:S(2)}, u32[]{:S(2)}) collective-permute-start(f32[3,48,256]{2,1,0:T(8,128)S(1)} %slice.25), channel_id=1, source_target_pairs={{0,4},{4,0},{8,12},{12,8},{16,20},{20,16},{24,28},{28,24},{1,5},{5... | collective-permute-start | bytes 442376 | tf_op jit(solution)/shard_map/ppermute | solution.py:145
  4.0 5.8 %collective-permute-start.1 = (f32[2,48,256]{2,1,0:T(8,128)S(1)}, f32[2,48,256]{2,1,0:T(8,128)S(1)}, u32[]{:S(2)}, u32[]{:S(2)}) collective-permute-start(f32[2,48,256]{2,1,0:T(8,128)S(1)} %slice.27), channel_id=1, source_target_pairs={{0,12},{4,8},{8,28},{12,24},{24,20},{28,16},{16,4},{20,0},{1,13},{... | collective-permute-start | bytes 294920 | tf_op jit(solution)/shard_map/ppermute | solution.py:146
  6.7 3.9 %collective-permute-start.2 = (f32[48,256]{1,0:T(8,128)S(1)}, f32[48,256]{1,0:T(8,128)S(1)}, u32[]{:S(2)}, u32[]{:S(2)}) collective-permute-start(f32[48,256]{1,0:T(8,128)S(1)} %get-tuple-element.9), channel_id=1, source_target_pairs={{0,20},{4,16},{8,4},{12,0},{24,12},{28,8},{16,28},{20,24},{1,21},{... | collective-permute-start | bytes 147464 | tf_op jit(solution)/shard_map/ppermute | solution.py:148
  7.7 4.4 %collective-permute-start.4 = (f32[48,256]{1,0:T(8,128)S(1)}, f32[48,256]{1,0:T(8,128)S(1)}, u32[]{:S(2)}, u32[]{:S(2)}) collective-permute-start(f32[48,256]{1,0:T(8,128)S(1)} %get-tuple-element.10), channel_id=1, source_target_pairs={{0,28},{4,24},{8,20},{12,16},{24,4},{28,0},{16,12},{20,8},{1,29},{... | collective-permute-start | bytes 147464 | tf_op jit(solution)/shard_map/ppermute | solution.py:148
  10.6 1.6 %collective-permute-start.3 = (f32[48,256]{1,0:T(8,128)S(1)}, f32[48,256]{1,0:T(8,128)S(1)}, u32[]{:S(2)}, u32[]{:S(2)}) collective-permute-start(f32[48,256]{1,0:T(8,128)S(1)} %dynamic-slice_bitcast_fusion), channel_id=1, source_target_pairs={{0,4},{4,0},{8,12},{12,8},{16,20},{20,16},{24,28},{28,24},{1,5},{5... | collective-permute-start | bytes 147464 | tf_op jit(solution)/shard_map/ppermute | solution.py:154
  12.2 5.3 %collective-permute-start.5 = (f32[48,256]{1,0:T(8,128)S(1)}, f32[48,256]{1,0:T(8,128)S(1)}, u32[]{:S(2)}, u32[]{:S(2)}) collective-permute-start(f32[48,256]{1,0:T(8,128)S(1)} %fusion.3), channel_id=1, source_target_pairs={{0,22},{1,7},{2,4},{3,5},{4,18},{5,3},{6,0},{7,1},{8,30},{9,15},{1... | collective-permute-start | bytes 147464 | tf_op jit(solution)/shard_map/ppermute | solution.py:162
  15.7 1.8 %collective-permute-start.6 = (f32[48,256]{1,0:T(8,128)S(1)}, f32[48,256]{1,0:T(8,128)S(1)}, u32[]{:S(2)}, u32[]{:S(2)}) collective-permute-start(f32[48,256]{1,0:T(8,128)S(1)} %fusion.3), channel_id=1, source_target_pairs={{0,4},{1,21},{2,22},{3,23},{4,0},{5,17},{6,18},{7,19},{8,12},{9,29... | collective-permute-start | bytes 147464 | tf_op jit(solution)/shard_map/ppermute | solution.py:163

commit v7 on v6

--- a/solution.py
+++ b/solution.py
@@ -8,6 +8,7 @@
 from jax.sharding import PartitionSpec as P
 
 CHUNK = 512
+DEPTH = 256
 MIB = 1 << 20
 
 
@@ -60,8 +61,17 @@
             at = end
         b_high, b_low = split(jnp.concatenate(pieces, axis=0))
         a_high, a_low = split(amp[:, start:start + size])
-        wide = dot(a_high, jnp.concatenate([b_high, b_low], axis=1))
-        total += wide[:, :cols] + wide[:, cols:] + dot(a_low, b_high)
+        b_both = jnp.concatenate([b_high, b_low], axis=1)
+        full = size - size % DEPTH
+        spare = size - full
+        if full and 2 * spare == DEPTH:
+            b_spare = jnp.concatenate([b_high[full:], jnp.zeros_like(b_low[full:])], axis=1)
+            wide = dot(jnp.concatenate([a_high, a_low[:, full:]], axis=1), jnp.concatenate([b_both, b_spare], axis=0))
+            low = dot(a_low[:, :full], b_high[:full])
+        else:
+            wide = dot(a_high, b_both)
+            low = dot(a_low, b_high)
+        total += wide[:, :cols] + wide[:, cols:] + low
     turned = total.T
     block = out_ref.shape[-2]
     for b in range(cols // block):

time: 18.3 us -> 18.3 us (level)
  no operation moved by 1% of the time
where the time goes in v7:
time: 18.3 us; the launch traced here: 18.1 us
  starting transfers between devices  9.72 us (53%)
  waiting for transfers between devices  4.17 us (23%)
  Pallas kernels  4.1 us (22%)
    ppermute x1, starting transfers between devices, shards(): turned = lax.ppermute(reduced, ('virt', 'pair'), across)  3.52 us
    pallas_call x1, Pallas kernels, ladder(): pl.pallas_call(functools.partial(ladder_kernel, place), out_shape=jax.Sha...  3.37 us
    ppermute x2, starting transfers between devices, shards(): lax.ppermute(mine[step - 1], 'virt', route(step))  2.76 us
    ppermute x1, starting transfers between devices, shards(): early = lax.ppermute(blocks[2 * rest:], 'virt', route(1))  2.65 us
    ppermute x2, waiting for transfers between devices, shards(): lax.ppermute(mine[step - 1], 'virt', route(step))  2.21 us
    ppermute x1, waiting for transfers between devices, shards(): turned = lax.ppermute(reduced, ('virt', 'pair'), across)  1.59 us
    pallas_call x1, Pallas kernels, finish(): pl.pallas_call(finish_kernel, out_shape=jax.ShapeDtypeStruct(own.shape, o...  0.73 us
    ppermute x1, starting transfers between devices, shards(): arrived = lax.ppermute(blocks[rest:2 * rest], 'virt', swap)  0.52 us
  transfers between devices with their start and end apart: 7, of which 4 were waited for; matrix products, arithmetic and copies ran while one was open for 0% of the time, Pallas kernels for 0%

profile of v7, /device:TPU:0, one launch (start us, length us, event | category | flops | bytes accessed | tf_op | source)
XLA Modules:
  0.0 18.1 jit_solution(2842876874954358211)
XLA Ops:
  0.0 0.0 copy-start
  0.0 3.4 %ladder.1 = f32[8,48,256]{2,1,0:T(8,128)S(1)} custom-call(s32[4,20]{1,0:T(4,128)} %bitcast.18, f32[256,1920]{1,0:T(8,128)} %amp_hbm.1, f32[1920,384]{1,0:T(8,128)} %int_hbm.1), custom_call_target="tpu_custom_call" | custom-call | tf_op jit(solution)/shard_map/ladder/pallas_call | solution.py:87
  3.4 0.5 %collective-permute-start = (f32[3,48,256]{2,1,0:T(8,128)S(1)}, f32[3,48,256]{2,1,0:T(8,128)S(1)}, u32[]{:S(2)}, u32[]{:S(2)}) collective-permute-start(f32[3,48,256]{2,1,0:T(8,128)S(1)} %slice.25), channel_id=1, source_target_pairs={{0,4},{4,0},{8,12},{12,8},{16,20},{20,16},{24,28},{28,24},{1,5},{5... | collective-permute-start | bytes 442376 | tf_op jit(solution)/shard_map/ppermute | solution.py:155
  3.9 2.6 %collective-permute-start.1 = (f32[2,48,256]{2,1,0:T(8,128)S(1)}, f32[2,48,256]{2,1,0:T(8,128)S(1)}, u32[]{:S(2)}, u32[]{:S(2)}) collective-permute-start(f32[2,48,256]{2,1,0:T(8,128)S(1)} %slice.27), channel_id=1, source_target_pairs={{0,12},{4,8},{8,28},{12,24},{24,20},{28,16},{16,4},{20,0},{1,13},{... | collective-permute-start | bytes 294920 | tf_op jit(solution)/shard_map/ppermute | solution.py:156
  6.6 0.0 collective-permute-done
  6.6 1.0 %collective-permute-start.2 = (f32[48,256]{1,0:T(8,128)S(1)}, f32[48,256]{1,0:T(8,128)S(1)}, u32[]{:S(2)}, u32[]{:S(2)}) collective-permute-start(f32[48,256]{1,0:T(8,128)S(1)} %get-tuple-element.9), channel_id=1, source_target_pairs={{0,20},{4,16},{8,4},{12,0},{24,12},{28,8},{16,28},{20,24},{1,21},{... | collective-permute-start | bytes 147464 | tf_op jit(solution)/shard_map/ppermute | solution.py:158
  7.6 1.7 %collective-permute-start.4 = (f32[48,256]{1,0:T(8,128)S(1)}, f32[48,256]{1,0:T(8,128)S(1)}, u32[]{:S(2)}, u32[]{:S(2)}) collective-permute-start(f32[48,256]{1,0:T(8,128)S(1)} %get-tuple-element.10), channel_id=1, source_target_pairs={{0,28},{4,24},{8,20},{12,16},{24,4},{28,0},{16,12},{20,8},{1,29},{... | collective-permute-start | bytes 147464 | tf_op jit(solution)/shard_map/ppermute | solution.py:158
  9.4 0.4 %collective-permute-done.1 = f32[2,48,256]{2,1,0:T(8,128)S(1)} collective-permute-done((f32[2,48,256]{2,1,0:T(8,128)S(1)}, f32[2,48,256]{2,1,0:T(8,128)S(1)}, u32[]{:S(2)}, u32[]{:S(2)}) %collective-permute-start.1) | collective-permute-done | bytes 98336 | tf_op jit(solution)/shard_map/ppermute | solution.py:156
  9.7 0.8 %collective-permute-done.2 = f32[48,256]{1,0:T(8,128)S(1)} collective-permute-done((f32[48,256]{1,0:T(8,128)S(1)}, f32[48,256]{1,0:T(8,128)S(1)}, u32[]{:S(2)}, u32[]{:S(2)}) %collective-permute-start.2) | collective-permute-done | bytes 49184 | tf_op jit(solution)/shard_map/ppermute | solution.py:158
  10.5 0.1 collective-permute-start.3
  10.6 1.4 %collective-permute-done.4 = f32[48,256]{1,0:T(8,128)S(1)} collective-permute-done((f32[48,256]{1,0:T(8,128)S(1)}, f32[48,256]{1,0:T(8,128)S(1)}, u32[]{:S(2)}, u32[]{:S(2)}) %collective-permute-start.4) | collective-permute-done | bytes 49184 | tf_op jit(solution)/shard_map/ppermute | solution.py:158
  12.1 0.0 collective-permute-done.3
  12.1 3.5 %collective-permute-start.5 = (f32[48,256]{1,0:T(8,128)S(1)}, f32[48,256]{1,0:T(8,128)S(1)}, u32[]{:S(2)}, u32[]{:S(2)}) collective-permute-start(f32[48,256]{1,0:T(8,128)S(1)} %fusion.3), channel_id=1, source_target_pairs={{0,22},{1,7},{2,4},{3,5},{4,18},{5,3},{6,0},{7,1},{8,30},{9,15},{1... | collective-permute-start | bytes 147464 | tf_op jit(solution)/shard_map/ppermute | solution.py:172
  15.6 0.2 collective-permute-start.6
  15.8 1.6 %collective-permute-done.5.other_ref = f32[48,256]{1,0:T(8,128)S(1)} collective-permute-done((f32[48,256]{1,0:T(8,128)S(1)}, f32[48,256]{1,0:T(8,128)S(1)}, u32[]{:S(2)}, u32[]{:S(2)}) %collective-permute-start.5) | collective-permute-done | bytes 49184 | tf_op jit(solution)/shard_map/ppermute | solution.py:172
  17.4 0.0 collective-permute-done.6.own_ref
  17.4 0.0 copy-done
  17.4 0.7 %finish.1 = f32[48,256]{1,0:T(8,128)} custom-call(s32[1,256]{1,0:T(1,128)S(1)} %bitcast.17, f32[48,256]{1,0:T(8,128)S(1)} %collective-permute-done.5.other_ref, f32[48,256]{1,0:T(8,128)S(1)} %collective-permute-done.6.own_ref), custom_call_target="tpu_custom_call" | custom-call | tf_op jit(solution)/shard_map/finish/pallas_call | solution.py:118
  (6 shorter events, 0.1 us)
Async XLA Ops:
  0.0 17.4 %copy-start = (s32[256]{0:T(256)S(1)}, s32[256]{0:T(256)}, u32[]{:S(2)}) copy-start(s32[256]{0:T(256)} %param.7) | copy-start | bytes 3076
  3.4 3.2 %collective-permute-start = (f32[3,48,256]{2,1,0:T(8,128)S(1)}, f32[3,48,256]{2,1,0:T(8,128)S(1)}, u32[]{:S(2)}, u32[]{:S(2)}) collective-permute-start(f32[3,48,256]{2,1,0:T(8,128)S(1)} %slice.25), channel_id=1, source_target_pairs={{0,4},{4,0},{8,12},{12,8},{16,20},{20,16},{24,28},{28,24},{1,5},{5... | collective-permute-start | bytes 442376 | tf_op jit(solution)/shard_map/ppermute | solution.py:155
  3.9 5.8 %collective-permute-start.1 = (f32[2,48,256]{2,1,0:T(8,128)S(1)}, f32[2,48,256]{2,1,0:T(8,128)S(1)}, u32[]{:S(2)}, u32[]{:S(2)}) collective-permute-start(f32[2,48,256]{2,1,0:T(8,128)S(1)} %slice.27), channel_id=1, source_target_pairs={{0,12},{4,8},{8,28},{12,24},{24,20},{28,16},{16,4},{20,0},{1,13},{... | collective-permute-start | bytes 294920 | tf_op jit(solution)/shard_map/ppermute | solution.py:156
  6.6 3.9 %collective-permute-start.2 = (f32[48,256]{1,0:T(8,128)S(1)}, f32[48,256]{1,0:T(8,128)S(1)}, u32[]{:S(2)}, u32[]{:S(2)}) collective-permute-start(f32[48,256]{1,0:T(8,128)S(1)} %get-tuple-element.9), channel_id=1, source_target_pairs={{0,20},{4,16},{8,4},{12,0},{24,12},{28,8},{16,28},{20,24},{1,21},{... | collective-permute-start | bytes 147464 | tf_op jit(solution)/shard_map/ppermute | solution.py:158
  7.6 4.4 %collective-permute-start.4 = (f32[48,256]{1,0:T(8,128)S(1)}, f32[48,256]{1,0:T(8,128)S(1)}, u32[]{:S(2)}, u32[]{:S(2)}) collective-permute-start(f32[48,256]{1,0:T(8,128)S(1)} %get-tuple-element.10), channel_id=1, source_target_pairs={{0,28},{4,24},{8,20},{12,16},{24,4},{28,0},{16,12},{20,8},{1,29},{... | collective-permute-start | bytes 147464 | tf_op jit(solution)/shard_map/ppermute | solution.py:158
  10.5 1.6 %collective-permute-start.3 = (f32[48,256]{1,0:T(8,128)S(1)}, f32[48,256]{1,0:T(8,128)S(1)}, u32[]{:S(2)}, u32[]{:S(2)}) collective-permute-start(f32[48,256]{1,0:T(8,128)S(1)} %dynamic-slice_bitcast_fusion), channel_id=1, source_target_pairs={{0,4},{4,0},{8,12},{12,8},{16,20},{20,16},{24,28},{28,24},{1,5},{5... | collective-permute-start | bytes 147464 | tf_op jit(solution)/shard_map/ppermute | solution.py:164
  12.1 5.3 %collective-permute-start.5 = (f32[48,256]{1,0:T(8,128)S(1)}, f32[48,256]{1,0:T(8,128)S(1)}, u32[]{:S(2)}, u32[]{:S(2)}) collective-permute-start(f32[48,256]{1,0:T(8,128)S(1)} %fusion.3), channel_id=1, source_target_pairs={{0,22},{1,7},{2,4},{3,5},{4,18},{5,3},{6,0},{7,1},{8,30},{9,15},{1... | collective-permute-start | bytes 147464 | tf_op jit(solution)/shard_map/ppermute | solution.py:172
  15.6 1.8 %collective-permute-start.6 = (f32[48,256]{1,0:T(8,128)S(1)}, f32[48,256]{1,0:T(8,128)S(1)}, u32[]{:S(2)}, u32[]{:S(2)}) collective-permute-start(f32[48,256]{1,0:T(8,128)S(1)} %fusion.3), channel_id=1, source_target_pairs={{0,4},{1,21},{2,22},{3,23},{4,0},{5,17},{6,18},{7,19},{8,12},{9,29... | collective-permute-start | bytes 147464 | tf_op jit(solution)/shard_map/ppermute | solution.py:173

commit v8 on v7

--- a/solution.py
+++ b/solution.py
@@ -152,16 +152,17 @@
 
     swap = [(i, i ^ 1) for i in range(n)]
     blocks = ladder(n, place, tile_mask.T, amplitudes, integrals)
-    arrived = lax.ppermute(blocks[rest:2 * rest], "virt", swap)
+    mine = []
+    if rest > 1:
+        mine = blocks[1:rest] + lax.ppermute(blocks[rest + 1:2 * rest], "virt", swap)
     early = lax.ppermute(blocks[2 * rest:], "virt", route(1))
-    mine = blocks[:rest] + arrived
-    came = [lax.ppermute(mine[step - 1], "virt", route(step)) for step in range(2, chips)]
+    came = [lax.ppermute(mine[step - 2], "virt", route(step)) for step in range(2, chips)]
     if came:
         early, came[0] = lax.optimization_barrier((early, came[0]))
     side = lax.axis_index("virt") % 2
     keep = lax.dynamic_index_in_dim(early, 1 - side, 0, keepdims=False)
     give = lax.dynamic_index_in_dim(early, side, 0, keepdims=False)
-    reduced = mine[0] + keep + lax.ppermute(give, "virt", swap)
+    reduced = blocks[0] + keep + lax.ppermute(give + blocks[rest], "virt", swap)
     for block in came:
         reduced = reduced + block
     def owner(i, q):

time: 18.3 us -> 18.2 us (level)
  no operation moved by 1% of the time
where the time goes in v8:
time: 18.2 us; the launch traced here: 18 us
  starting transfers between devices  9.74 us (54%)
  Pallas kernels  4.1 us (23%)
  waiting for transfers between devices  4.09 us (22%)
    ppermute x1, starting transfers between devices, shards(): turned = lax.ppermute(reduced, ('virt', 'pair'), across)  3.52 us
    pallas_call x1, Pallas kernels, ladder(): pl.pallas_call(functools.partial(ladder_kernel, place), out_shape=jax.Sha...  3.37 us
    ppermute x2, starting transfers between devices, shards(): lax.ppermute(mine[step - 2], 'virt', route(step))  2.76 us
    ppermute x1, starting transfers between devices, shards(): early = lax.ppermute(blocks[2 * rest:], 'virt', route(1))  2.6 us
    ppermute x2, waiting for transfers between devices, shards(): lax.ppermute(mine[step - 2], 'virt', route(step))  2.16 us
    ppermute x1, waiting for transfers between devices, shards(): turned = lax.ppermute(reduced, ('virt', 'pair'), across)  1.59 us
    pallas_call x1, Pallas kernels, finish(): pl.pallas_call(finish_kernel, out_shape=jax.ShapeDtypeStruct(own.shape, o...  0.73 us
    ppermute x1, starting transfers between devices, shards(): lax.ppermute(blocks[rest + 1:2 * rest], 'virt', swap)  0.52 us
  transfers between devices with their start and end apart: 7, of which 4 were waited for; matrix products, arithmetic and copies ran while one was open for 0% of the time, Pallas kernels for 0%

profile of v8, /device:TPU:0, one launch (start us, length us, event | category | flops | bytes accessed | tf_op | source)
XLA Modules:
  0.0 18.0 jit_solution(12390290669727588743)
XLA Ops:
  0.0 0.0 copy-start
  0.0 3.4 %ladder.1 = f32[8,48,256]{2,1,0:T(8,128)S(1)} custom-call(s32[4,20]{1,0:T(4,128)} %bitcast.18, f32[256,1920]{1,0:T(8,128)} %amp_hbm.1, f32[1920,384]{1,0:T(8,128)} %int_hbm.1), custom_call_target="tpu_custom_call" | custom-call | tf_op jit(solution)/shard_map/ladder/pallas_call | solution.py:87
  3.4 0.5 %collective-permute-start.1 = (f32[2,48,256]{2,1,0:T(8,128)S(1)}, f32[2,48,256]{2,1,0:T(8,128)S(1)}, u32[]{:S(2)}, u32[]{:S(2)}) collective-permute-start(f32[2,48,256]{2,1,0:T(8,128)S(1)} %get-tuple-element.10), channel_id=1, source_target_pairs={{0,4},{4,0},{8,12},{12,8},{16,20},{20,16},{24,28},{28,24},{1,5},{5... | collective-permute-start | bytes 294920 | tf_op jit(solution)/shard_map/ppermute | solution.py:157
  3.9 2.6 %collective-permute-start = (f32[2,48,256]{2,1,0:T(8,128)S(1)}, f32[2,48,256]{2,1,0:T(8,128)S(1)}, u32[]{:S(2)}, u32[]{:S(2)}) collective-permute-start(f32[2,48,256]{2,1,0:T(8,128)S(1)} %get-tuple-element.9), channel_id=1, source_target_pairs={{0,12},{4,8},{8,28},{12,24},{24,20},{28,16},{16,4},{20,0},{1,13},{... | collective-permute-start | bytes 294920 | tf_op jit(solution)/shard_map/ppermute | solution.py:158
  6.5 0.0 collective-permute-done.1
  6.6 1.0 %collective-permute-start.2 = (f32[48,256]{1,0:T(8,128)S(1)}, f32[48,256]{1,0:T(8,128)S(1)}, u32[]{:S(2)}, u32[]{:S(2)}) collective-permute-start(f32[48,256]{1,0:T(8,128)S(1)} %get-tuple-element.11), channel_id=1, source_target_pairs={{0,20},{4,16},{8,4},{12,0},{24,12},{28,8},{16,28},{20,24},{1,21},{... | collective-permute-start | bytes 147464 | tf_op jit(solution)/shard_map/ppermute | solution.py:159
  7.6 1.7 %collective-permute-start.4 = (f32[48,256]{1,0:T(8,128)S(1)}, f32[48,256]{1,0:T(8,128)S(1)}, u32[]{:S(2)}, u32[]{:S(2)}) collective-permute-start(f32[48,256]{1,0:T(8,128)S(1)} %get-tuple-element.12), channel_id=1, source_target_pairs={{0,28},{4,24},{8,20},{12,16},{24,4},{28,0},{16,12},{20,8},{1,29},{... | collective-permute-start | bytes 147464 | tf_op jit(solution)/shard_map/ppermute | solution.py:159
  9.3 0.3 %collective-permute-done = f32[2,48,256]{2,1,0:T(8,128)S(1)} collective-permute-done((f32[2,48,256]{2,1,0:T(8,128)S(1)}, f32[2,48,256]{2,1,0:T(8,128)S(1)}, u32[]{:S(2)}, u32[]{:S(2)}) %collective-permute-start) | collective-permute-done | bytes 98336 | tf_op jit(solution)/shard_map/ppermute | solution.py:158
  9.7 0.8 %collective-permute-done.2 = f32[48,256]{1,0:T(8,128)S(1)} collective-permute-done((f32[48,256]{1,0:T(8,128)S(1)}, f32[48,256]{1,0:T(8,128)S(1)}, u32[]{:S(2)}, u32[]{:S(2)}) %collective-permute-start.2) | collective-permute-done | bytes 49184 | tf_op jit(solution)/shard_map/ppermute | solution.py:159
  10.4 0.2 %collective-permute-start.3 = (f32[48,256]{1,0:T(8,128)S(1)}, f32[48,256]{1,0:T(8,128)S(1)}, u32[]{:S(2)}, u32[]{:S(2)}) collective-permute-start(f32[48,256]{1,0:T(8,128)S(1)} %fusion), channel_id=1, source_target_pairs={{0,4},{4,0},{8,12},{12,8},{16,20},{20,16},{24,28},{28,24},{1,5},{5... | collective-permute-start | bytes 147464 | tf_op jit(solution)/shard_map/ppermute | solution.py:165
  10.6 1.4 %collective-permute-done.4 = f32[48,256]{1,0:T(8,128)S(1)} collective-permute-done((f32[48,256]{1,0:T(8,128)S(1)}, f32[48,256]{1,0:T(8,128)S(1)}, u32[]{:S(2)}, u32[]{:S(2)}) %collective-permute-start.4) | collective-permute-done | bytes 49184 | tf_op jit(solution)/shard_map/ppermute | solution.py:159
  12.0 0.0 collective-permute-done.3
  12.0 3.5 %collective-permute-start.5 = (f32[48,256]{1,0:T(8,128)S(1)}, f32[48,256]{1,0:T(8,128)S(1)}, u32[]{:S(2)}, u32[]{:S(2)}) collective-permute-start(f32[48,256]{1,0:T(8,128)S(1)} %fusion.4), channel_id=1, source_target_pairs={{0,22},{1,7},{2,4},{3,5},{4,18},{5,3},{6,0},{7,1},{8,30},{9,15},{1... | collective-permute-start | bytes 147464 | tf_op jit(solution)/shard_map/ppermute | solution.py:173
  15.6 0.2 collective-permute-start.6
  15.7 1.6 %collective-permute-done.5.other_ref = f32[48,256]{1,0:T(8,128)S(1)} collective-permute-done((f32[48,256]{1,0:T(8,128)S(1)}, f32[48,256]{1,0:T(8,128)S(1)}, u32[]{:S(2)}, u32[]{:S(2)}) %collective-permute-start.5) | collective-permute-done | bytes 49184 | tf_op jit(solution)/shard_map/ppermute | solution.py:173
  17.3 0.0 collective-permute-done.6.own_ref
  17.3 0.0 copy-done
  17.3 0.7 %finish.1 = f32[48,256]{1,0:T(8,128)} custom-call(s32[1,256]{1,0:T(1,128)S(1)} %bitcast.17, f32[48,256]{1,0:T(8,128)S(1)} %collective-permute-done.5.other_ref, f32[48,256]{1,0:T(8,128)S(1)} %collective-permute-done.6.own_ref), custom_call_target="tpu_custom_call" | custom-call | tf_op jit(solution)/shard_map/finish/pallas_call | solution.py:118
  (5 shorter events, 0.1 us)
Async XLA Ops:
  0.0 17.3 %copy-start = (s32[256]{0:T(256)S(1)}, s32[256]{0:T(256)}, u32[]{:S(2)}) copy-start(s32[256]{0:T(256)} %param.7) | copy-start | bytes 3076
  3.4 3.1 %collective-permute-start.1 = (f32[2,48,256]{2,1,0:T(8,128)S(1)}, f32[2,48,256]{2,1,0:T(8,128)S(1)}, u32[]{:S(2)}, u32[]{:S(2)}) collective-permute-start(f32[2,48,256]{2,1,0:T(8,128)S(1)} %get-tuple-element.10), channel_id=1, source_target_pairs={{0,4},{4,0},{8,12},{12,8},{16,20},{20,16},{24,28},{28,24},{1,5},{5... | collective-permute-start | bytes 294920 | tf_op jit(solution)/shard_map/ppermute | solution.py:157
  3.9 5.7 %collective-permute-start = (f32[2,48,256]{2,1,0:T(8,128)S(1)}, f32[2,48,256]{2,1,0:T(8,128)S(1)}, u32[]{:S(2)}, u32[]{:S(2)}) collective-permute-start(f32[2,48,256]{2,1,0:T(8,128)S(1)} %get-tuple-element.9), channel_id=1, source_target_pairs={{0,12},{4,8},{8,28},{12,24},{24,20},{28,16},{16,4},{20,0},{1,13},{... | collective-permute-start | bytes 294920 | tf_op jit(solution)/shard_map/ppermute | solution.py:158
  6.6 3.8 %collective-permute-start.2 = (f32[48,256]{1,0:T(8,128)S(1)}, f32[48,256]{1,0:T(8,128)S(1)}, u32[]{:S(2)}, u32[]{:S(2)}) collective-permute-start(f32[48,256]{1,0:T(8,128)S(1)} %get-tuple-element.11), channel_id=1, source_target_pairs={{0,20},{4,16},{8,4},{12,0},{24,12},{28,8},{16,28},{20,24},{1,21},{... | collective-permute-start | bytes 147464 | tf_op jit(solution)/shard_map/ppermute | solution.py:159
  7.6 4.4 %collective-permute-start.4 = (f32[48,256]{1,0:T(8,128)S(1)}, f32[48,256]{1,0:T(8,128)S(1)}, u32[]{:S(2)}, u32[]{:S(2)}) collective-permute-start(f32[48,256]{1,0:T(8,128)S(1)} %get-tuple-element.12), channel_id=1, source_target_pairs={{0,28},{4,24},{8,20},{12,16},{24,4},{28,0},{16,12},{20,8},{1,29},{... | collective-permute-start | bytes 147464 | tf_op jit(solution)/shard_map/ppermute | solution.py:159
  10.4 1.6 %collective-permute-start.3 = (f32[48,256]{1,0:T(8,128)S(1)}, f32[48,256]{1,0:T(8,128)S(1)}, u32[]{:S(2)}, u32[]{:S(2)}) collective-permute-start(f32[48,256]{1,0:T(8,128)S(1)} %fusion), channel_id=1, source_target_pairs={{0,4},{4,0},{8,12},{12,8},{16,20},{20,16},{24,28},{28,24},{1,5},{5... | collective-permute-start | bytes 147464 | tf_op jit(solution)/shard_map/ppermute | solution.py:165
  12.0 5.3 %collective-permute-start.5 = (f32[48,256]{1,0:T(8,128)S(1)}, f32[48,256]{1,0:T(8,128)S(1)}, u32[]{:S(2)}, u32[]{:S(2)}) collective-permute-start(f32[48,256]{1,0:T(8,128)S(1)} %fusion.4), channel_id=1, source_target_pairs={{0,22},{1,7},{2,4},{3,5},{4,18},{5,3},{6,0},{7,1},{8,30},{9,15},{1... | collective-permute-start | bytes 147464 | tf_op jit(solution)/shard_map/ppermute | solution.py:173
  15.6 1.8 %collective-permute-start.6 = (f32[48,256]{1,0:T(8,128)S(1)}, f32[48,256]{1,0:T(8,128)S(1)}, u32[]{:S(2)}, u32[]{:S(2)}) collective-permute-start(f32[48,256]{1,0:T(8,128)S(1)} %fusion.4), channel_id=1, source_target_pairs={{0,4},{1,21},{2,22},{3,23},{4,0},{5,17},{6,18},{7,19},{8,12},{9,29... | collective-permute-start | bytes 147464 | tf_op jit(solution)/shard_map/ppermute | solution.py:174

commit v9 on v8

--- a/solution.py
+++ b/solution.py
@@ -25,7 +25,6 @@
 
 def ladder_kernel(place, mask_hbm, amp_hbm, int_hbm, out_ref, mask_ref, amp, ints, sems, small_sem):
     depth, cols = int_hbm.shape
-    rows = amp_hbm.shape[0]
     spans = chunks_of(depth)
     small = pltpu.make_async_copy(mask_hbm, mask_ref, small_sem)
     large = []
@@ -43,7 +42,7 @@
     col_tiles, tile_rows = mask_ref.shape
     tile_r, tile_c = depth // tile_rows, cols // col_tiles
     lane = lax.broadcasted_iota(jnp.int32, (1, cols), 1)
-    total = jnp.zeros((rows, cols), jnp.float32)
+    total = None
     small.wait()
     dot = functools.partial(jnp.dot, preferred_element_type=jnp.float32)
     for (start, size), pair in zip(spans, large):
@@ -71,7 +70,8 @@
         else:
             wide = dot(a_high, b_both)
             low = dot(a_low, b_high)
-        total += wide[:, :cols] + wide[:, cols:] + low
+        part = wide[:, :cols] + wide[:, cols:] + low
+        total = part if total is None else total + part
     turned = total.T
     block = out_ref.shape[-2]
     for b in range(cols // block):

time: 18.2 us -> 18.2 us (level)
  no operation moved by 1% of the time
where the time goes in v9:
time: 18.2 us; the launch traced here: 18 us
  starting transfers between devices  9.74 us (54%)
  Pallas kernels  4.1 us (23%)
  waiting for transfers between devices  4.09 us (22%)
    ppermute x1, starting transfers between devices, shards(): turned = lax.ppermute(reduced, ('virt', 'pair'), across)  3.52 us
    pallas_call x1, Pallas kernels, ladder(): pl.pallas_call(functools.partial(ladder_kernel, place), out_shape=jax.Sha...  3.37 us
    ppermute x2, starting transfers between devices, shards(): lax.ppermute(mine[step - 2], 'virt', route(step))  2.76 us
    ppermute x1, starting transfers between devices, shards(): early = lax.ppermute(blocks[2 * rest:], 'virt', route(1))  2.6 us
    ppermute x2, waiting for transfers between devices, shards(): lax.ppermute(mine[step - 2], 'virt', route(step))  2.16 us
    ppermute x1, waiting for transfers between devices, shards(): turned = lax.ppermute(reduced, ('virt', 'pair'), across)  1.59 us
    pallas_call x1, Pallas kernels, finish(): pl.pallas_call(finish_kernel, out_shape=jax.ShapeDtypeStruct(own.shape, o...  0.73 us
    ppermute x1, starting transfers between devices, shards(): lax.ppermute(blocks[rest + 1:2 * rest], 'virt', swap)  0.52 us
  transfers between devices with their start and end apart: 7, of which 4 were waited for; matrix products, arithmetic and copies ran while one was open for 0% of the time, Pallas kernels for 0%

profile of v9, /device:TPU:0, one launch (start us, length us, event | category | flops | bytes accessed | tf_op | source)
XLA Modules:
  0.0 18.0 jit_solution(12390290669727588743)
XLA Ops:
  0.0 0.0 copy-start
  0.0 3.4 %ladder.1 = f32[8,48,256]{2,1,0:T(8,128)S(1)} custom-call(s32[4,20]{1,0:T(4,128)} %bitcast.18, f32[256,1920]{1,0:T(8,128)} %amp_hbm.1, f32[1920,384]{1,0:T(8,128)} %int_hbm.1), custom_call_target="tpu_custom_call" | custom-call | tf_op jit(solution)/shard_map/ladder/pallas_call | solution.py:87
  3.4 0.5 %collective-permute-start.1 = (f32[2,48,256]{2,1,0:T(8,128)S(1)}, f32[2,48,256]{2,1,0:T(8,128)S(1)}, u32[]{:S(2)}, u32[]{:S(2)}) collective-permute-start(f32[2,48,256]{2,1,0:T(8,128)S(1)} %get-tuple-element.10), channel_id=1, source_target_pairs={{0,4},{4,0},{8,12},{12,8},{16,20},{20,16},{24,28},{28,24},{1,5},{5... | collective-permute-start | bytes 294920 | tf_op jit(solution)/shard_map/ppermute | solution.py:157
  3.9 2.6 %collective-permute-start = (f32[2,48,256]{2,1,0:T(8,128)S(1)}, f32[2,48,256]{2,1,0:T(8,128)S(1)}, u32[]{:S(2)}, u32[]{:S(2)}) collective-permute-start(f32[2,48,256]{2,1,0:T(8,128)S(1)} %get-tuple-element.9), channel_id=1, source_target_pairs={{0,12},{4,8},{8,28},{12,24},{24,20},{28,16},{16,4},{20,0},{1,13},{... | collective-permute-start | bytes 294920 | tf_op jit(solution)/shard_map/ppermute | solution.py:158
  6.5 0.0 collective-permute-done.1
  6.6 1.0 %collective-permute-start.2 = (f32[48,256]{1,0:T(8,128)S(1)}, f32[48,256]{1,0:T(8,128)S(1)}, u32[]{:S(2)}, u32[]{:S(2)}) collective-permute-start(f32[48,256]{1,0:T(8,128)S(1)} %get-tuple-element.11), channel_id=1, source_target_pairs={{0,20},{4,16},{8,4},{12,0},{24,12},{28,8},{16,28},{20,24},{1,21},{... | collective-permute-start | bytes 147464 | tf_op jit(solution)/shard_map/ppermute | solution.py:159
  7.6 1.7 %collective-permute-start.4 = (f32[48,256]{1,0:T(8,128)S(1)}, f32[48,256]{1,0:T(8,128)S(1)}, u32[]{:S(2)}, u32[]{:S(2)}) collective-permute-start(f32[48,256]{1,0:T(8,128)S(1)} %get-tuple-element.12), channel_id=1, source_target_pairs={{0,28},{4,24},{8,20},{12,16},{24,4},{28,0},{16,12},{20,8},{1,29},{... | collective-permute-start | bytes 147464 | tf_op jit(solution)/shard_map/ppermute | solution.py:159
  9.3 0.3 %collective-permute-done = f32[2,48,256]{2,1,0:T(8,128)S(1)} collective-permute-done((f32[2,48,256]{2,1,0:T(8,128)S(1)}, f32[2,48,256]{2,1,0:T(8,128)S(1)}, u32[]{:S(2)}, u32[]{:S(2)}) %collective-permute-start) | collective-permute-done | bytes 98336 | tf_op jit(solution)/shard_map/ppermute | solution.py:158
  9.7 0.8 %collective-permute-done.2 = f32[48,256]{1,0:T(8,128)S(1)} collective-permute-done((f32[48,256]{1,0:T(8,128)S(1)}, f32[48,256]{1,0:T(8,128)S(1)}, u32[]{:S(2)}, u32[]{:S(2)}) %collective-permute-start.2) | collective-permute-done | bytes 49184 | tf_op jit(solution)/shard_map/ppermute | solution.py:159
  10.4 0.2 %collective-permute-start.3 = (f32[48,256]{1,0:T(8,128)S(1)}, f32[48,256]{1,0:T(8,128)S(1)}, u32[]{:S(2)}, u32[]{:S(2)}) collective-permute-start(f32[48,256]{1,0:T(8,128)S(1)} %fusion), channel_id=1, source_target_pairs={{0,4},{4,0},{8,12},{12,8},{16,20},{20,16},{24,28},{28,24},{1,5},{5... | collective-permute-start | bytes 147464 | tf_op jit(solution)/shard_map/ppermute | solution.py:165
  10.6 1.4 %collective-permute-done.4 = f32[48,256]{1,0:T(8,128)S(1)} collective-permute-done((f32[48,256]{1,0:T(8,128)S(1)}, f32[48,256]{1,0:T(8,128)S(1)}, u32[]{:S(2)}, u32[]{:S(2)}) %collective-permute-start.4) | collective-permute-done | bytes 49184 | tf_op jit(solution)/shard_map/ppermute | solution.py:159
  12.0 0.0 collective-permute-done.3
  12.0 3.5 %collective-permute-start.5 = (f32[48,256]{1,0:T(8,128)S(1)}, f32[48,256]{1,0:T(8,128)S(1)}, u32[]{:S(2)}, u32[]{:S(2)}) collective-permute-start(f32[48,256]{1,0:T(8,128)S(1)} %fusion.4), channel_id=1, source_target_pairs={{0,22},{1,7},{2,4},{3,5},{4,18},{5,3},{6,0},{7,1},{8,30},{9,15},{1... | collective-permute-start | bytes 147464 | tf_op jit(solution)/shard_map/ppermute | solution.py:173
  15.6 0.2 collective-permute-start.6
  15.7 1.6 %collective-permute-done.5.other_ref = f32[48,256]{1,0:T(8,128)S(1)} collective-permute-done((f32[48,256]{1,0:T(8,128)S(1)}, f32[48,256]{1,0:T(8,128)S(1)}, u32[]{:S(2)}, u32[]{:S(2)}) %collective-permute-start.5) | collective-permute-done | bytes 49184 | tf_op jit(solution)/shard_map/ppermute | solution.py:173
  17.3 0.0 collective-permute-done.6.own_ref
  17.3 0.0 copy-done
  17.3 0.7 %finish.1 = f32[48,256]{1,0:T(8,128)} custom-call(s32[1,256]{1,0:T(1,128)S(1)} %bitcast.17, f32[48,256]{1,0:T(8,128)S(1)} %collective-permute-done.5.other_ref, f32[48,256]{1,0:T(8,128)S(1)} %collective-permute-done.6.own_ref), custom_call_target="tpu_custom_call" | custom-call | tf_op jit(solution)/shard_map/finish/pallas_call | solution.py:118
  (5 shorter events, 0.1 us)
Async XLA Ops:
  0.0 17.3 %copy-start = (s32[256]{0:T(256)S(1)}, s32[256]{0:T(256)}, u32[]{:S(2)}) copy-start(s32[256]{0:T(256)} %param.7) | copy-start | bytes 3076
  3.4 3.1 %collective-permute-start.1 = (f32[2,48,256]{2,1,0:T(8,128)S(1)}, f32[2,48,256]{2,1,0:T(8,128)S(1)}, u32[]{:S(2)}, u32[]{:S(2)}) collective-permute-start(f32[2,48,256]{2,1,0:T(8,128)S(1)} %get-tuple-element.10), channel_id=1, source_target_pairs={{0,4},{4,0},{8,12},{12,8},{16,20},{20,16},{24,28},{28,24},{1,5},{5... | collective-permute-start | bytes 294920 | tf_op jit(solution)/shard_map/ppermute | solution.py:157
  3.9 5.7 %collective-permute-start = (f32[2,48,256]{2,1,0:T(8,128)S(1)}, f32[2,48,256]{2,1,0:T(8,128)S(1)}, u32[]{:S(2)}, u32[]{:S(2)}) collective-permute-start(f32[2,48,256]{2,1,0:T(8,128)S(1)} %get-tuple-element.9), channel_id=1, source_target_pairs={{0,12},{4,8},{8,28},{12,24},{24,20},{28,16},{16,4},{20,0},{1,13},{... | collective-permute-start | bytes 294920 | tf_op jit(solution)/shard_map/ppermute | solution.py:158
  6.6 3.8 %collective-permute-start.2 = (f32[48,256]{1,0:T(8,128)S(1)}, f32[48,256]{1,0:T(8,128)S(1)}, u32[]{:S(2)}, u32[]{:S(2)}) collective-permute-start(f32[48,256]{1,0:T(8,128)S(1)} %get-tuple-element.11), channel_id=1, source_target_pairs={{0,20},{4,16},{8,4},{12,0},{24,12},{28,8},{16,28},{20,24},{1,21},{... | collective-permute-start | bytes 147464 | tf_op jit(solution)/shard_map/ppermute | solution.py:159
  7.6 4.4 %collective-permute-start.4 = (f32[48,256]{1,0:T(8,128)S(1)}, f32[48,256]{1,0:T(8,128)S(1)}, u32[]{:S(2)}, u32[]{:S(2)}) collective-permute-start(f32[48,256]{1,0:T(8,128)S(1)} %get-tuple-element.12), channel_id=1, source_target_pairs={{0,28},{4,24},{8,20},{12,16},{24,4},{28,0},{16,12},{20,8},{1,29},{... | collective-permute-start | bytes 147464 | tf_op jit(solution)/shard_map/ppermute | solution.py:159
  10.4 1.6 %collective-permute-start.3 = (f32[48,256]{1,0:T(8,128)S(1)}, f32[48,256]{1,0:T(8,128)S(1)}, u32[]{:S(2)}, u32[]{:S(2)}) collective-permute-start(f32[48,256]{1,0:T(8,128)S(1)} %fusion), channel_id=1, source_target_pairs={{0,4},{4,0},{8,12},{12,8},{16,20},{20,16},{24,28},{28,24},{1,5},{5... | collective-permute-start | bytes 147464 | tf_op jit(solution)/shard_map/ppermute | solution.py:165
  12.0 5.3 %collective-permute-start.5 = (f32[48,256]{1,0:T(8,128)S(1)}, f32[48,256]{1,0:T(8,128)S(1)}, u32[]{:S(2)}, u32[]{:S(2)}) collective-permute-start(f32[48,256]{1,0:T(8,128)S(1)} %fusion.4), channel_id=1, source_target_pairs={{0,22},{1,7},{2,4},{3,5},{4,18},{5,3},{6,0},{7,1},{8,30},{9,15},{1... | collective-permute-start | bytes 147464 | tf_op jit(solution)/shard_map/ppermute | solution.py:173
  15.6 1.8 %collective-permute-start.6 = (f32[48,256]{1,0:T(8,128)S(1)}, f32[48,256]{1,0:T(8,128)S(1)}, u32[]{:S(2)}, u32[]{:S(2)}) collective-permute-start(f32[48,256]{1,0:T(8,128)S(1)} %fusion.4), channel_id=1, source_target_pairs={{0,4},{1,21},{2,22},{3,23},{4,0},{5,17},{6,18},{7,19},{8,12},{9,29... | collective-permute-start | bytes 147464 | tf_op jit(solution)/shard_map/ppermute | solution.py:174

commit v10 on v9

--- a/solution.py
+++ b/solution.py
@@ -129,7 +129,7 @@
     n, g = lax.axis_size("virt"), lax.axis_size("pair")
     chips = n // 2
     rest = chips - 1
-    ring = [i ^ (i >> 1) for i in range(chips)]
+    ring = [i ^ (i >> 1) for i in (-p % chips for p in range(chips))]
     if sorted(ring) != list(range(chips)):
         ring = list(range(chips))
     distances = [d for near in range(1, chips // 2 + 1) for d in (near, chips - near)][:rest]

time: 18.2 us -> 18.2 us (level)
  starting transfers between devices: 9.74 us -> 9.32 us
  waiting for transfers between devices: 4.09 us -> 4.46 us
    ppermute x1, starting transfers between devices: 3.52 us -> 3.1 us  [shards(): turned = lax.ppermute(reduced, ('virt', 'pair'), across)]
    ppermute x2, waiting for transfers between devices: 2.16 us -> 2.56 us  [shards(): lax.ppermute(mine[step - 2], 'virt', route(step))]
where the time goes in v10:
time: 18.2 us; the launch traced here: 18 us
  starting transfers between devices  9.32 us (51%)
  waiting for transfers between devices  4.46 us (25%)
  Pallas kernels  4.1 us (23%)
    pallas_call x1, Pallas kernels, ladder(): pl.pallas_call(functools.partial(ladder_kernel, place), out_shape=jax.Sha...  3.37 us
    ppermute x1, starting transfers between devices, shards(): turned = lax.ppermute(reduced, ('virt', 'pair'), across)  3.1 us
    ppermute x2, starting transfers between devices, shards(): lax.ppermute(mine[step - 2], 'virt', route(step))  2.73 us
    ppermute x1, starting transfers between devices, shards(): early = lax.ppermute(blocks[2 * rest:], 'virt', route(1))  2.63 us
    ppermute x2, waiting for transfers between devices, shards(): lax.ppermute(mine[step - 2], 'virt', route(step))  2.56 us
    ppermute x1, waiting for transfers between devices, shards(): turned = lax.ppermute(reduced, ('virt', 'pair'), across)  1.59 us
    pallas_call x1, Pallas kernels, finish(): pl.pallas_call(finish_kernel, out_shape=jax.ShapeDtypeStruct(own.shape, o...  0.73 us
    ppermute x1, starting transfers between devices, shards(): lax.ppermute(blocks[rest + 1:2 * rest], 'virt', swap)  0.52 us
  transfers between devices with their start and end apart: 7, of which 4 were waited for; matrix products, arithmetic and copies ran while one was open for 0% of the time, Pallas kernels for 0%

profile of v10, /device:TPU:0, one launch (start us, length us, event | category | flops | bytes accessed | tf_op | source)
XLA Modules:
  0.0 18.0 jit_solution(17648872513315563891)
XLA Ops:
  0.0 0.0 copy-start
  0.0 3.4 %ladder.1 = f32[8,48,256]{2,1,0:T(8,128)S(1)} custom-call(s32[4,20]{1,0:T(4,128)} %bitcast.18, f32[256,1920]{1,0:T(8,128)} %amp_hbm.1, f32[1920,384]{1,0:T(8,128)} %int_hbm.1), custom_call_target="tpu_custom_call" | custom-call | tf_op jit(solution)/shard_map/ladder/pallas_call | solution.py:87
  3.4 0.5 %collective-permute-start.1 = (f32[2,48,256]{2,1,0:T(8,128)S(1)}, f32[2,48,256]{2,1,0:T(8,128)S(1)}, u32[]{:S(2)}, u32[]{:S(2)}) collective-permute-start(f32[2,48,256]{2,1,0:T(8,128)S(1)} %get-tuple-element.10), channel_id=1, source_target_pairs={{0,4},{4,0},{8,12},{12,8},{16,20},{20,16},{24,28},{28,24},{1,5},{5... | collective-permute-start | bytes 294920 | tf_op jit(solution)/shard_map/ppermute | solution.py:157
  3.9 2.6 %collective-permute-start = (f32[2,48,256]{2,1,0:T(8,128)S(1)}, f32[2,48,256]{2,1,0:T(8,128)S(1)}, u32[]{:S(2)}, u32[]{:S(2)}) collective-permute-start(f32[2,48,256]{2,1,0:T(8,128)S(1)} %get-tuple-element.9), channel_id=1, source_target_pairs={{0,20},{4,16},{16,28},{20,24},{24,12},{28,8},{8,4},{12,0},{1,21},{... | collective-permute-start | bytes 294920 | tf_op jit(solution)/shard_map/ppermute | solution.py:158
  6.6 0.0 collective-permute-done.1
  6.6 1.0 %collective-permute-start.2 = (f32[48,256]{1,0:T(8,128)S(1)}, f32[48,256]{1,0:T(8,128)S(1)}, u32[]{:S(2)}, u32[]{:S(2)}) collective-permute-start(f32[48,256]{1,0:T(8,128)S(1)} %get-tuple-element.11), channel_id=1, source_target_pairs={{0,12},{4,8},{16,4},{20,0},{24,20},{28,16},{8,28},{12,24},{1,13},{... | collective-permute-start | bytes 147464 | tf_op jit(solution)/shard_map/ppermute | solution.py:159
  7.6 1.8 %collective-permute-start.4 = (f32[48,256]{1,0:T(8,128)S(1)}, f32[48,256]{1,0:T(8,128)S(1)}, u32[]{:S(2)}, u32[]{:S(2)}) collective-permute-start(f32[48,256]{1,0:T(8,128)S(1)} %get-tuple-element.12), channel_id=1, source_target_pairs={{0,28},{4,24},{16,12},{20,8},{24,4},{28,0},{8,20},{12,16},{1,29},{... | collective-permute-start | bytes 147464 | tf_op jit(solution)/shard_map/ppermute | solution.py:159
  9.3 0.3 %collective-permute-done = f32[2,48,256]{2,1,0:T(8,128)S(1)} collective-permute-done((f32[2,48,256]{2,1,0:T(8,128)S(1)}, f32[2,48,256]{2,1,0:T(8,128)S(1)}, u32[]{:S(2)}, u32[]{:S(2)}) %collective-permute-start) | collective-permute-done | bytes 98336 | tf_op jit(solution)/shard_map/ppermute | solution.py:158
  9.6 0.8 %collective-permute-done.2 = f32[48,256]{1,0:T(8,128)S(1)} collective-permute-done((f32[48,256]{1,0:T(8,128)S(1)}, f32[48,256]{1,0:T(8,128)S(1)}, u32[]{:S(2)}, u32[]{:S(2)}) %collective-permute-start.2) | collective-permute-done | bytes 49184 | tf_op jit(solution)/shard_map/ppermute | solution.py:159
  10.4 0.2 %collective-permute-start.3 = (f32[48,256]{1,0:T(8,128)S(1)}, f32[48,256]{1,0:T(8,128)S(1)}, u32[]{:S(2)}, u32[]{:S(2)}) collective-permute-start(f32[48,256]{1,0:T(8,128)S(1)} %fusion), channel_id=1, source_target_pairs={{0,4},{4,0},{8,12},{12,8},{16,20},{20,16},{24,28},{28,24},{1,5},{5... | collective-permute-start | bytes 147464 | tf_op jit(solution)/shard_map/ppermute | solution.py:165
  10.6 1.7 %collective-permute-done.4 = f32[48,256]{1,0:T(8,128)S(1)} collective-permute-done((f32[48,256]{1,0:T(8,128)S(1)}, f32[48,256]{1,0:T(8,128)S(1)}, u32[]{:S(2)}, u32[]{:S(2)}) %collective-permute-start.4) | collective-permute-done | bytes 49184 | tf_op jit(solution)/shard_map/ppermute | solution.py:159
  12.4 0.0 collective-permute-done.3
  12.4 3.1 %collective-permute-start.5 = (f32[48,256]{1,0:T(8,128)S(1)}, f32[48,256]{1,0:T(8,128)S(1)}, u32[]{:S(2)}, u32[]{:S(2)}) collective-permute-start(f32[48,256]{1,0:T(8,128)S(1)} %fusion.4), channel_id=1, source_target_pairs={{0,22},{1,7},{2,4},{3,5},{4,18},{5,3},{6,0},{7,1},{8,30},{9,15},{1... | collective-permute-start | bytes 147464 | tf_op jit(solution)/shard_map/ppermute | solution.py:173
  15.5 0.2 collective-permute-start.6
  15.7 1.6 %collective-permute-done.5.other_ref = f32[48,256]{1,0:T(8,128)S(1)} collective-permute-done((f32[48,256]{1,0:T(8,128)S(1)}, f32[48,256]{1,0:T(8,128)S(1)}, u32[]{:S(2)}, u32[]{:S(2)}) %collective-permute-start.5) | collective-permute-done | bytes 49184 | tf_op jit(solution)/shard_map/ppermute | solution.py:173
  17.3 0.0 collective-permute-done.6.own_ref
  17.3 0.0 copy-done
  17.3 0.7 %finish.1 = f32[48,256]{1,0:T(8,128)} custom-call(s32[1,256]{1,0:T(1,128)S(1)} %bitcast.17, f32[48,256]{1,0:T(8,128)S(1)} %collective-permute-done.5.other_ref, f32[48,256]{1,0:T(8,128)S(1)} %collective-permute-done.6.own_ref), custom_call_target="tpu_custom_call" | custom-call | tf_op jit(solution)/shard_map/finish/pallas_call | solution.py:118
  (5 shorter events, 0.1 us)
Async XLA Ops:
  0.0 17.3 %copy-start = (s32[256]{0:T(256)S(1)}, s32[256]{0:T(256)}, u32[]{:S(2)}) copy-start(s32[256]{0:T(256)} %param.7) | copy-start | bytes 3076
  3.4 3.2 %collective-permute-start.1 = (f32[2,48,256]{2,1,0:T(8,128)S(1)}, f32[2,48,256]{2,1,0:T(8,128)S(1)}, u32[]{:S(2)}, u32[]{:S(2)}) collective-permute-start(f32[2,48,256]{2,1,0:T(8,128)S(1)} %get-tuple-element.10), channel_id=1, source_target_pairs={{0,4},{4,0},{8,12},{12,8},{16,20},{20,16},{24,28},{28,24},{1,5},{5... | collective-permute-start | bytes 294920 | tf_op jit(solution)/shard_map/ppermute | solution.py:157
  3.9 5.7 %collective-permute-start = (f32[2,48,256]{2,1,0:T(8,128)S(1)}, f32[2,48,256]{2,1,0:T(8,128)S(1)}, u32[]{:S(2)}, u32[]{:S(2)}) collective-permute-start(f32[2,48,256]{2,1,0:T(8,128)S(1)} %get-tuple-element.9), channel_id=1, source_target_pairs={{0,20},{4,16},{16,28},{20,24},{24,12},{28,8},{8,4},{12,0},{1,21},{... | collective-permute-start | bytes 294920 | tf_op jit(solution)/shard_map/ppermute | solution.py:158
  6.6 3.8 %collective-permute-start.2 = (f32[48,256]{1,0:T(8,128)S(1)}, f32[48,256]{1,0:T(8,128)S(1)}, u32[]{:S(2)}, u32[]{:S(2)}) collective-permute-start(f32[48,256]{1,0:T(8,128)S(1)} %get-tuple-element.11), channel_id=1, source_target_pairs={{0,12},{4,8},{16,4},{20,0},{24,20},{28,16},{8,28},{12,24},{1,13},{... | collective-permute-start | bytes 147464 | tf_op jit(solution)/shard_map/ppermute | solution.py:159
  7.6 4.8 %collective-permute-start.4 = (f32[48,256]{1,0:T(8,128)S(1)}, f32[48,256]{1,0:T(8,128)S(1)}, u32[]{:S(2)}, u32[]{:S(2)}) collective-permute-start(f32[48,256]{1,0:T(8,128)S(1)} %get-tuple-element.12), channel_id=1, source_target_pairs={{0,28},{4,24},{16,12},{20,8},{24,4},{28,0},{8,20},{12,16},{1,29},{... | collective-permute-start | bytes 147464 | tf_op jit(solution)/shard_map/ppermute | solution.py:159
  10.4 1.9 %collective-permute-start.3 = (f32[48,256]{1,0:T(8,128)S(1)}, f32[48,256]{1,0:T(8,128)S(1)}, u32[]{:S(2)}, u32[]{:S(2)}) collective-permute-start(f32[48,256]{1,0:T(8,128)S(1)} %fusion), channel_id=1, source_target_pairs={{0,4},{4,0},{8,12},{12,8},{16,20},{20,16},{24,28},{28,24},{1,5},{5... | collective-permute-start | bytes 147464 | tf_op jit(solution)/shard_map/ppermute | solution.py:165
  12.4 4.9 %collective-permute-start.5 = (f32[48,256]{1,0:T(8,128)S(1)}, f32[48,256]{1,0:T(8,128)S(1)}, u32[]{:S(2)}, u32[]{:S(2)}) collective-permute-start(f32[48,256]{1,0:T(8,128)S(1)} %fusion.4), channel_id=1, source_target_pairs={{0,22},{1,7},{2,4},{3,5},{4,18},{5,3},{6,0},{7,1},{8,30},{9,15},{1... | collective-permute-start | bytes 147464 | tf_op jit(solution)/shard_map/ppermute | solution.py:173
  15.5 1.8 %collective-permute-start.6 = (f32[48,256]{1,0:T(8,128)S(1)}, f32[48,256]{1,0:T(8,128)S(1)}, u32[]{:S(2)}, u32[]{:S(2)}) collective-permute-start(f32[48,256]{1,0:T(8,128)S(1)} %fusion.4), channel_id=1, source_target_pairs={{0,4},{1,21},{2,22},{3,23},{4,0},{5,17},{6,18},{7,19},{8,12},{9,29... | collective-permute-start | bytes 147464 | tf_op jit(solution)/shard_map/ppermute | solution.py:174
